TPU v7x, 32 devices: a whole 2x2x4 slice. The times are simulated.
32 devices in a mesh: dom: 8 (over z, y), sub: 4 (over x, core).
Axes of the slice: x: 2, y: 2, z: 4, core: 2. Of those that a mesh axis runs over, the one named last changes fastest.
Arguments:
- positions: float32 [3, 65536], P(None, ('dom', 'sub')), may hold values from -6 to 6
- fixed_mask: int32 [65536], P(('dom', 'sub')), may hold values 0 or 1
- send_count: int32 [8, 4, 5, 4], P('dom', 'sub'), may hold values from 0 to 128, as said below
- send_list: int32 [8, 4, 5, 4, 128], P('dom', 'sub'), may hold values from 0 to 2047, as said below
- block_nodes: int32 [64, 4096], P(None, ('dom', 'sub')), may hold values from 0 to 4607, as said below
- tet_corners: int32 [4, 524288], P(None, ('dom', 'sub')), may hold values from 0 to 63, as said below
Outputs:
- smoothed: float32 [3, 65536], P(None, ('dom', 'sub'))
Inputs may be any that keep to these rules, and one draw needn't show every extreme that they name: send_count[d, s, k, t] is the number of nodes that partition (d, s) sends to the partition at dom index (d + k - 2) modulo the dom axis's size and sub index t; it is zero for k = 2, t = s. send_list[d, s, k, t, j] for j below send_count[d, s, k, t] is the local index of an owned node of partition (d, s), sent to that neighbour's ghost slot (k, s, j); later entries are ignored. `block_nodes`: entries are local columns of the block's partition: below 2048 an owned node, else 2048 + (k * 4 + t) * 128 + j for a ghost slot whose j is below the sending partition's count. `tet_corners`: the four corners of a tetrahedron are distinct rows.
All inputs are finite; a program needn't handle non-finite values. No bound on the sum of `fixed_mask` on one device may be relied on, other than what follows from the above.
Results may differ from a plain program's by a relative error of at most 0.0003.
Values sent between devices are 32-bit elements; how exact they have to be, the bound alone decides.
No kernel may reach another device: no remote copies, remote signals or barrier semaphores. Data moves between devices by JAX's collectives and lax.ppermute only.
A program may use at most 128 MiB of HBM per device.

v0:
```python
import math

import jax
import jax.numpy as jnp
from jax import lax
from jax.sharding import PartitionSpec as P

ITERS = 2


delta_reg = 2.0
step_size = 0.01
winv_rows = (
    (1.0, -1.0 / math.sqrt(3.0), -1.0 / math.sqrt(6.0)),
    (0.0, 2.0 / math.sqrt(3.0), -1.0 / math.sqrt(6.0)),
    (0.0, 0.0, math.sqrt(1.5)),
)


def distortion_sum(corners):
    edge_rows = [[corners[r, m + 1] - corners[r, 0] for m in range(3)] for r in range(3)]
    shape_mat = []
    for r in range(3):
        row_vals = []
        for c in range(3):
            acc_val = None
            for m in range(3):
                if winv_rows[m][c] != 0.0:
                    term_val = edge_rows[r][m] * winv_rows[m][c]
                    acc_val = term_val if acc_val is None else acc_val + term_val
            row_vals.append(acc_val)
        shape_mat.append(row_vals)
    norm_sq = shape_mat[0][0] * shape_mat[0][0]
    for r in range(3):
        for c in range(3):
            if r + c > 0:
                norm_sq = norm_sq + shape_mat[r][c] * shape_mat[r][c]
    volume_det = (
        shape_mat[0][0] * (shape_mat[1][1] * shape_mat[2][2] - shape_mat[1][2] * shape_mat[2][1])
        - shape_mat[0][1] * (shape_mat[1][0] * shape_mat[2][2] - shape_mat[1][2] * shape_mat[2][0])
        + shape_mat[0][2] * (shape_mat[1][0] * shape_mat[2][1] - shape_mat[1][1] * shape_mat[2][0])
    )
    root_term = jnp.sqrt(volume_det * volume_det + 4.0 * delta_reg * delta_reg)
    upper_part = 0.5 * (volume_det + root_term)
    lower_den = jnp.where(volume_det < 0, root_term - volume_det, 1.0)
    height = jnp.where(volume_det >= 0, upper_part, 2.0 * delta_reg * delta_reg / lower_den)
    distortion = norm_sq / (3.0 * height ** (2.0 / 3.0))
    return jnp.sum(distortion)


def tet_energy(local_nodes, block_nodes, tet_corners):
    block_count = block_nodes.shape[1]
    group_size = math.gcd(block_count, 16)
    group_count = block_count // group_size
    block_coords = local_nodes[:, block_nodes.T]
    block_coords = block_coords.reshape(3, group_count, group_size, 64).transpose(1, 0, 2, 3)
    corner_rows = tet_corners.reshape(4, group_count, group_size, 128).transpose(1, 0, 2, 3)
    column_ids = jnp.arange(64, dtype=jnp.int32)

    def group_energy(item):
        coords, rows = item
        incidence = (rows[:, :, :, None] == column_ids[None, None, None, :]).astype(jnp.float32)
        corners = jnp.einsum("rgm,ngim->rngi", coords, incidence, precision=lax.Precision.HIGHEST)
        return distortion_sum(corners)

    return jnp.sum(lax.map(group_energy, (block_coords, corner_rows)))


def coalesced_forward(payload, dom_here, dom_count, reach_doms):
    slot_ids = jnp.arange(payload.shape[1], dtype=jnp.int32)
    targets = (dom_here + slot_ids - reach_doms) % dom_count
    padded = jnp.zeros((3, payload.shape[2], dom_count, payload.shape[3]), jnp.float32)
    padded = padded.at[:, :, targets, :].set(payload.transpose(0, 2, 1, 3))
    received = lax.all_to_all(
        lax.all_to_all(padded, "dom", split_axis=2, concat_axis=2, tiled=True),
        "sub",
        split_axis=1,
        concat_axis=1,
        tiled=True,
    )
    sources = (dom_here - slot_ids + reach_doms) % dom_count
    return received[:, :, sources, :].transpose(0, 2, 1, 3)


def coalesced_back(ghost_grad, dom_here, dom_count, reach_doms):
    slot_ids = jnp.arange(ghost_grad.shape[1], dtype=jnp.int32)
    targets = (dom_here - slot_ids + reach_doms) % dom_count
    padded = jnp.zeros((3, ghost_grad.shape[2], dom_count, ghost_grad.shape[3]), jnp.float32)
    padded = padded.at[:, :, targets, :].set(ghost_grad.transpose(0, 2, 1, 3))
    received = lax.all_to_all(
        lax.all_to_all(padded, "dom", split_axis=2, concat_axis=2, tiled=True),
        "sub",
        split_axis=1,
        concat_axis=1,
        tiled=True,
    )
    sources = (dom_here + slot_ids - reach_doms) % dom_count
    return received[:, :, sources, :].transpose(0, 2, 1, 3)


def per_device(positions, fixed_mask, send_count, send_list, block_nodes, tet_corners):
    node_count = positions.shape[1]
    slot_count = send_list.shape[2]
    sub_count = send_list.shape[3]
    slot_width = send_list.shape[4]
    reach_doms = (slot_count - 1) // 2
    dom_count = lax.axis_size("dom")
    dom_here = lax.axis_index("dom")
    counts = send_count[0, 0]
    send_rows = send_list[0, 0]
    slot_index = jnp.arange(slot_width, dtype=jnp.int32)
    valid_mask = slot_index[None, None, :] < counts[:, :, None]
    flat_rows = send_rows.reshape(-1)
    free_nodes = (fixed_mask == 0).astype(jnp.float32)
    grad_fn = jax.grad(tet_energy)
    owned_pos = positions
    for step in range(ITERS):
        picked = owned_pos[:, send_rows]
        payload = jnp.where(valid_mask[None], picked, 0.0)
        ghosts = coalesced_forward(payload, dom_here, dom_count, reach_doms)
        local_nodes = jnp.concatenate([owned_pos, ghosts.reshape(3, -1)], axis=1)
        local_grad = grad_fn(local_nodes, block_nodes, tet_corners)
        ghost_grad = local_grad[:, node_count:].reshape(3, slot_count, sub_count, slot_width)
        returned = coalesced_back(ghost_grad, dom_here, dom_count, reach_doms)
        returned = jnp.where(valid_mask[None], returned, 0.0)
        grad_total = local_grad[:, :node_count].at[:, flat_rows].add(returned.reshape(3, -1))
        owned_pos = owned_pos - step_size * free_nodes[None, :] * grad_total
    return owned_pos


def solution(mesh):
    return jax.shard_map(
        per_device,
        mesh=mesh,
        in_specs=(
            P(None, ("dom", "sub")),
            P(("dom", "sub")),
            P("dom", "sub", None, None),
            P("dom", "sub", None, None, None),
            P(None, ("dom", "sub")),
            P(None, ("dom", "sub")),
        ),
        out_specs=P(None, ("dom", "sub")),
        check_vma=False,
    )
```

profile of v0, /device:TPU:0, one launch (start us, length us, event | category | flops | bytes accessed | tf_op | source)
XLA Modules:
  0.0 566.3 jit_solution(13838661475403771654)
XLA Ops:
  2.0 4.1 gather_fusion
  8.2 7.3 %all-to-all-start = ((f32[3,4,8,128]{3,1,0,2:T(4,128)}), f32[3,4,8,128]{3,1,0,2:T(4,128)S(1)}, u32[]{:S(2)}, u32[]{:S(2)}) async-start(f32[3,4,8,128]{3,1,0,2:T(4,128)} %copy.376), calls=%async_computation | async-start | bytes 98304 | tf_op jit(solution)/shard_map/all_to_all | solution.py:75
  17.2 5.2 all-to-all-done
  26.3 3.9 all-to-all-done.1
  31.6 27.7 %gather_fusion.2 = f32[8192,3]{1,0:T(8,128)} fusion(f32[3,4608]{0,1:T(8,128)S(1)} %copy.380, s32[8192]{0:T(1024)S(1)} %broadcast_clamp_fusion), kind=kCustom, calls=%fused_computation.2 | custom fusion | bytes 229376 | tf_op jit(solution)/shard_map/jvp()/gather | solution.py:55
  62.4 7.9 %broadcast.6321.clone2 = f32[8,4,16,128,64]{3,4,1,2,0:T(8,128)} broadcast(f32[]{:T(128)} %constant.498.clone.1), dimensions={} | broadcast | bytes 16777220 | tf_op jit(solution)/shard_map/broadcast.105
  76.6 85.8 %while.140 = (s32[]{:T(128)}, f32[8,4,16,128,64]{3,4,1,2,0:T(8,128)}, f32[8,16,128]{2,1,0:T(8,128)S(1)}, f32[8,16,128]{2,1,0:T(8,128)S(1)}, f32[8,16,128]{2,1,0:...) while((s32[]{:T(128)}, ...), condition=%wide.region_2.3_spmd.clone.clone, body=%wide.region_1.2_spmd.clone.clone.sunk | while | flops 20658176 | bytes 11524857 | solution.py:66
  163.1 46.5 %while.138 = (s32[]{:T(128)}, f32[8,3,16,64]{3,1,2,0:T(4,128)S(1)}, f32[8,16,128]{2,1,0:T(8,128)S(1)}, f32[8,16,128]{2,1,0:T(8,128)S(1)}, pred[8,16,128]{2,1,0:T...) while((s32[]{:T(128)}, f32[8,3,16,64]{3,1,2,0:T(4,128)S(1)}, ...), condition=%wide.region_4.5_spmd, body=%wide.region_3.4_spmd.sunk | while | flops 19525636 | bytes 3093761 | solution.py:66
  165.5 3.4 fusion.157
  171.3 3.4 fusion.157
  177.1 3.4 fusion.157
  182.9 3.4 fusion.157
  188.7 3.4 fusion.157
  194.5 3.4 fusion.157
  200.3 3.4 fusion.157
  206.1 3.4 fusion.157
  212.4 44.9 %scatter_custom_fusion.1 = f32[3,4608]{0,1:T(8,128)S(1)} fusion(s32[8192]{0:T(1024)S(1)} %reshape.10223, f32[8192,3]{1,0:T(8,128)} %bitcast.674, f32[]{:T(128)} %constant.498.clone.1), kind=kCustom, calls=%fused_computation.295 | custom fusion | flops 24576 | bytes 55808 | tf_op jit(solution)/shard_map/transpose(jvp())/scatter-add | solution.py:55
  265.6 6.1 %all-to-all-done.2 = f32[3,4,8,128]{3,1,0,2:T(4,128)S(1)} async-done(((f32[3,4,8,128]{3,1,0,2:T(4,128)}), f32[3,4,8,128]{3,1,0,2:T(4,128)S(1)}, u32[]{:S(2)}, u32[]{:S(2)}) %all-to-all-start.2) | async-done | bytes 49184 | tf_op jit(solution)/shard_map/all_to_all | solution.py:91
  281.5 14.9 %scatter_fusion.2 = f32[3,2048]{0,1:T(8,128)S(1)} fusion(f32[3,2048]{0,1:T(8,128)S(1)} %slice.236, s32[2560]{0:T(1024)} %fusion.96, f32[2560,3]{1,0:T(8,128)S(1)} %copy.391), kind=kCustom, calls=%fused_computation.11 | custom fusion | flops 7680 | bytes 102400 | tf_op jit(solution)/shard_map/scatter-add | solution.py:126
  297.2 4.1 gather_fusion.4
  302.6 9.2 %all_to_all.40 = f32[3,4,8,128]{3,1,0,2:T(4,128)S(1)} all-to-all(f32[3,4,8,128]{3,1,0,2:T(4,128)S(1)} %copy.395), channel_id=1, replica_groups=mesh['dom'=8,'sub'=4] {'dom'}, dimensions={2} | all-to-all | bytes 98304 | tf_op jit(solution)/shard_map/all_to_all | solution.py:75
  315.7 4.0 all-to-all-done.5
  323.4 27.7 %gather_fusion.6 = f32[8192,3]{1,0:T(8,128)} fusion(f32[3,4608]{0,1:T(8,128)S(1)} %pad_maximum_fusion, s32[8192]{0:T(1024)S(1)} %broadcast_clamp_fusion), kind=kCustom, calls=%fused_computation.6 | custom fusion | bytes 229376 | tf_op jit(solution)/shard_map/jvp()/gather | solution.py:55
  354.1 7.9 %broadcast.6321.clone = f32[8,4,16,128,64]{3,4,1,2,0:T(8,128)} broadcast(f32[]{:T(128)} %constant.498.clone.1), dimensions={} | broadcast | bytes 16777220 | tf_op jit(solution)/shard_map/broadcast.105
  363.5 82.7 %while.141 = (s32[]{:T(128)}, f32[8,4,16,128,64]{3,4,1,2,0:T(8,128)}, f32[8,16,128]{2,1,0:T(8,128)S(1)}, f32[8,16,128]{2,1,0:T(8,128)S(1)}, f32[8,16,128]{2,1,0:...) while((s32[]{:T(128)}, ...), condition=%wide.region_10.11_spmd.clone.clone, body=%wide.region_9.10_spmd.clone.clone.sunk | while | flops 20658176 | bytes 11523841 | solution.py:66
  446.2 34.6 %while.139 = (s32[]{:T(128)}, f32[8,3,16,64]{3,1,2,0:T(4,128)S(1)}, f32[8,16,128]{2,1,0:T(8,128)S(1)}, f32[8,16,128]{2,1,0:T(8,128)S(1)}, pred[8,16,128]{2,1,0:T...) while((s32[]{:T(128)}, f32[8,3,16,64]{3,1,2,0:T(4,128)S(1)}, ...), condition=%wide.region_12.13_spmd, body=%wide.region_11.12_spmd.sunk | while | flops 19525636 | bytes 3093761 | solution.py:66
  447.1 3.4 fusion.164
  451.4 3.4 fusion.164
  483.6 45.1 %scatter_custom_fusion.5 = f32[3,4608]{0,1:T(8,128)S(1)} fusion(s32[8192]{0:T(1024)} %copy-done.3, f32[8192,3]{1,0:T(8,128)} %bitcast.673, f32[]{:T(128)} %constant.498.clone.1), kind=kCustom, calls=%fused_computation.293 | custom fusion | flops 24576 | bytes 55808 | tf_op jit(solution)/shard_map/transpose(jvp())/scatter-add | solution.py:55
  532.4 9.2 %all_to_all.41 = f32[3,4,8,128]{3,1,0,2:T(4,128)S(1)} all-to-all(f32[3,4,8,128]{3,1,0,2:T(4,128)S(1)} %copy.406), channel_id=1, replica_groups=mesh['dom'=8,'sub'=4] {'dom'}, dimensions={2} | all-to-all | bytes 98304 | tf_op jit(solution)/shard_map/all_to_all | solution.py:91
  545.6 3.9 all-to-all-done.7
  550.8 14.6 %scatter_fusion.5 = f32[3,2048]{0,1:T(8,128)S(1)} fusion(f32[3,2048]{0,1:T(8,128)S(1)} %slice.238, s32[2560]{0:T(1024)S(1)} %copy-done.4, f32[2560,3]{1,0:T(8,128)S(1)} %copy.410), kind=kCustom, calls=%fused_computation.15 | custom fusion | flops 7680 | bytes 102400 | tf_op jit(solution)/shard_map/scatter-add | solution.py:126
  (481 shorter events, 282.2 us)
Async XLA Ops:
  0.0 6.6 %copy-start.14 = (s32[1,1,5,4]{2,3,1,0:T(4,128)S(1)}, s32[1,1,5,4]{2,3,1,0:T(4,128)}, u32[]{:S(2)}) copy-start(s32[1,1,5,4]{2,3,1,0:T(4,128)} %param.16) | copy-start | bytes 244
  0.0 15.5 %copy-start.10 = (s32[64,128]{1,0:T(8,128)S(1)}, s32[64,128]{1,0:T(8,128)}, u32[]{:S(2)}) copy-start(s32[64,128]{1,0:T(8,128)} %param.18) | copy-start | bytes 98308
  0.0 16.5 %copy-start.15 = (s32[2048]{0:T(1024)S(1)}, s32[2048]{0:T(1024)}, u32[]{:S(2)}) copy-start(s32[2048]{0:T(1024)} %param.15) | copy-start | bytes 24580
  0.0 26.3 %copy-start.2 = (s32[4,16384]{1,0:T(4,128)S(1)}, s32[4,16384]{1,0:T(4,128)}, u32[]{:S(2)}) copy-start(s32[4,16384]{1,0:T(4,128)} %param.19) | copy-start | bytes 786436
  0.0 8.2 %copy-start.19 = (s32[5]{0:T(128)}, s32[5]{0:T(128)S(1)}, u32[]{:S(2)}) copy-start(s32[5]{0:T(128)S(1)} %fusion.99) | copy-start | bytes 64
  0.8 5.9 %copy-start.5 = (s32[3072]{0:T(1024)}, s32[3072]{0:T(1024)S(1)}, u32[]{:S(2)}) copy-start(s32[3072]{0:T(1024)S(1)} %pad_clamp_fusion) | copy-start | bytes 36868
  0.8 30.1 %copy-start.1 = (f32[3,2048]{1,0:T(4,128)S(1)}, f32[3,2048]{1,0:T(4,128)}, u32[]{:S(2)}) copy-start(f32[3,2048]{1,0:T(4,128)} %param.14) | copy-start | bytes 73732
  6.7 1.5 copy-start.12
  8.2 14.1 %all-to-all-start = ((f32[3,4,8,128]{3,1,0,2:T(4,128)}), f32[3,4,8,128]{3,1,0,2:T(4,128)S(1)}, u32[]{:S(2)}, u32[]{:S(2)}) async-start(f32[3,4,8,128]{3,1,0,2:T(4,128)} %copy.376), calls=%async_computation | async-start | bytes 98304 | tf_op jit(solution)/shard_map/all_to_all | solution.py:75
  15.7 196.6 %copy-start.3 = (s32[8192]{0:T(1024)}, s32[8192]{0:T(1024)S(1)}, u32[]{:S(2)}) copy-start(s32[8192]{0:T(1024)S(1)} %reshape.10223) | copy-start | bytes 98308
  17.1 243.0 %copy-start.17 = (s32[5]{0:T(128)}, s32[5]{0:T(128)S(1)}, u32[]{:S(2)}) copy-start(s32[5]{0:T(128)S(1)} %fusion.100) | copy-start | bytes 64
  23.0 7.3 %all-to-all-start.1 = ((f32[3,4,8,128]{3,2,0,1:T(8,128)}), f32[3,4,8,128]{3,2,0,1:T(8,128)S(1)}, u32[]{:S(2)}, u32[]{:S(2)}) async-start(f32[3,4,8,128]{3,2,0,1:T(8,128)} %copy.377), calls=%async_computation.1 | async-start | bytes 98304 | tf_op jit(solution)/shard_map/all_to_all | solution.py:74
  26.3 33.1 %copy-start.16 = (s32[1024]{0:T(1024)}, s32[1024]{0:T(1024)S(1)}, u32[]{:S(2)}) copy-start(s32[1024]{0:T(1024)S(1)} %pad_clamp_fusion.2) | copy-start | bytes 12292
  162.4 0.7 copy-start
  257.3 7.7 %copy-start.9 = (s32[1,1,5,4,128]{4,3,2,1,0:T(4,128)S(1)}, s32[1,1,5,4,128]{4,3,2,1,0:T(4,128)}, u32[]{:S(2)}) copy-start(s32[1,1,5,4,128]{4,3,2,1,0:T(4,128)} %param.17) | copy-start | bytes 30724
  257.3 18.3 %copy-start.20 = (s32[5]{0:T(128)S(1)}, s32[5]{0:T(128)}, u32[]{:S(2)}) copy-start(s32[5]{0:T(128)} %copy-done.19) | copy-start | bytes 64
  261.6 10.1 %all-to-all-start.2 = ((f32[3,4,8,128]{3,1,0,2:T(4,128)}), f32[3,4,8,128]{3,1,0,2:T(4,128)S(1)}, u32[]{:S(2)}, u32[]{:S(2)}) async-start(f32[3,4,8,128]{3,1,0,2:T(4,128)} %copy.387), calls=%async_computation.2 | async-start | bytes 98304 | tf_op jit(solution)/shard_map/all_to_all | solution.py:91
  272.3 7.3 %all-to-all-start.3 = ((f32[3,4,8,128]{3,2,0,1:T(8,128)}), f32[3,4,8,128]{3,2,0,1:T(8,128)S(1)}, u32[]{:S(2)}, u32[]{:S(2)}) async-start(f32[3,4,8,128]{3,2,0,1:T(8,128)} %copy.388), calls=%async_computation.3 | async-start | bytes 98304 | tf_op jit(solution)/shard_map/all_to_all | solution.py:90
  276.3 20.5 %copy-start.7 = (f32[2048]{0:T(1024)S(1)}, f32[2048]{0:T(1024)}, u32[]{:S(2)}) copy-start(f32[2048]{0:T(1024)} %compare_select_fusion.3) | copy-start | bytes 24580
  276.3 20.9 %copy-start.6 = (s32[3072]{0:T(1024)S(1)}, s32[3072]{0:T(1024)}, u32[]{:S(2)}) copy-start(s32[3072]{0:T(1024)} %copy-done.5) | copy-start | bytes 36868
  281.5 20.2 %copy-start.13 = (pred[4,5,128]{2,0,1:T(4,128)(4,1)S(1)}, pred[4,5,128]{2,0,1:T(4,128)(4,1)}, u32[]{:S(2)}) copy-start(pred[4,5,128]{2,0,1:T(4,128)(4,1)} %copy-done.12) | copy-start | bytes 7684
  281.5 20.3 %copy-start.21 = (s32[5]{0:T(128)S(1)}, s32[5]{0:T(128)}, u32[]{:S(2)}) copy-start(s32[5]{0:T(128)} %copy-done.19) | copy-start | bytes 64
  312.4 7.3 %all-to-all-start.5 = ((f32[3,4,8,128]{3,2,0,1:T(8,128)}), f32[3,4,8,128]{3,2,0,1:T(8,128)S(1)}, u32[]{:S(2)}, u32[]{:S(2)}) async-start(f32[3,4,8,128]{3,2,0,1:T(8,128)} %copy.396), calls=%async_computation.5 | async-start | bytes 98304 | tf_op jit(solution)/shard_map/all_to_all | solution.py:74
  528.7 2.9 copy-start.18
  529.9 20.4 %copy-start.11 = (pred[5,4,128]{2,1,0:T(4,128)(4,1)S(1)}, pred[5,4,128]{2,1,0:T(4,128)(4,1)}, u32[]{:S(2)}) copy-start(pred[5,4,128]{2,1,0:T(4,128)(4,1)} %iota_compare_fusion.6) | copy-start | bytes 7684
  531.6 19.2 %copy-start.4 = (s32[2560]{0:T(1024)S(1)}, s32[2560]{0:T(1024)}, u32[]{:S(2)}) copy-start(s32[2560]{0:T(1024)} %fusion.96) | copy-start | bytes 30724
  542.2 7.3 %all-to-all-start.7 = ((f32[3,4,8,128]{3,2,0,1:T(8,128)}), f32[3,4,8,128]{3,2,0,1:T(8,128)S(1)}, u32[]{:S(2)}, u32[]{:S(2)}) async-start(f32[3,4,8,128]{3,2,0,1:T(8,128)} %copy.407), calls=%async_computation.7 | async-start | bytes 98304 | tf_op jit(solution)/shard_map/all_to_all | solution.py:90
  545.5 20.2 %copy-start.8 = (f32[2048]{0:T(1024)S(1)}, f32[2048]{0:T(1024)}, u32[]{:S(2)}) copy-start(f32[2048]{0:T(1024)} %compare_select_fusion.3) | copy-start | bytes 24580
where the time goes:
time: 571 us; the launch traced here: 566 us
  other arithmetic  226 us (40%)
  local copies, waits for them, and re-layouts  203 us (36%)
  matrix products  67.2 us (12%)
  waiting for transfers between devices  26.4 us (5%)
  starting transfers between devices  23.8 us (4%)
  blocking collectives  18.3 us (3%)
    scatter-add x2, other arithmetic, tet_energy(): block_coords = local_nodes[:, block_nodes.T]  90 us
    dynamic_update_slice x80, local copies, waits for them, and re-layouts, tet_energy(): return jnp.sum(lax.map(group_energy, (block_coords, corner_rows)))  74.3 us
    dot_general x32, matrix products, group_energy(): jnp.einsum('rgm,ngim->rngi', coords, incidence, precision=lax.Precision.H...  67.2 us
    gather x4, local copies, waits for them, and re-layouts, tet_energy(): block_coords = local_nodes[:, block_nodes.T]  61.4 us
    convert_element_type x16, other arithmetic, group_energy(): (rows[:, :, :, None] == column_ids[None, None, None, :]).astype(jnp.float32)  48.3 us
    scatter-add x2, other arithmetic, per_device(): local_grad[:, :node_count].at[:, flat_rows].add(returned.reshape(3, -1))  29.5 us
    dynamic_update_slice x64, other arithmetic, tet_energy(): return jnp.sum(lax.map(group_energy, (block_coords, corner_rows)))  26.1 us
    neg x64, other arithmetic, distortion_sum(): corners[r, m + 1] - corners[r, 0]  25.2 us
  transfers between devices with their start and end apart: 6, of which 6 were waited for; matrix products, arithmetic and copies ran while one was open for 1% of the time, Pallas kernels for 0%

commit v1 on v0

v1 whole, which is shorter than its diff:
```python
import functools
import math

import jax
import jax.numpy as jnp
from jax import lax
from jax.experimental import pallas as pl
from jax.experimental.pallas import tpu as pltpu
from jax.sharding import PartitionSpec as P

ITERS = 2
LANES = 128
BLOCK_ROWS = 64

delta_reg = 2.0
step_size = 0.01

LANE_GATHER = lax.GatherDimensionNumbers(
    offset_dims=(),
    collapsed_slice_dims=(1,),
    start_index_map=(1,),
    operand_batching_dims=(0,),
    start_indices_batching_dims=(0,),
)


def lane_gather(table, index):
    return lax.gather(
        table,
        index[:, :, None],
        LANE_GATHER,
        slice_sizes=(1, 1),
        mode=lax.GatherScatterMode.PROMISE_IN_BOUNDS,
    )


def row_iota(rows):
    return lax.broadcasted_iota(jnp.int32, (rows, LANES), 0).astype(jnp.float32).astype(jnp.bfloat16)


def row_equals(ids_row, rows):
    packed = jnp.broadcast_to(ids_row.astype(jnp.float32), (16, LANES)).astype(jnp.bfloat16)
    return jnp.concatenate([packed] * (rows // 16), axis=0) == row_iota(rows)


def one_hot(ids_row, rows):
    mask = row_equals(ids_row, rows)
    return jnp.where(mask, jnp.ones((rows, LANES), jnp.bfloat16), jnp.zeros((rows, LANES), jnp.bfloat16))


def split_two(values):
    upper = values.astype(jnp.bfloat16).astype(jnp.float32)
    return upper, values - upper


def masked_rows(mask, row):
    rows = mask.shape[0]
    packed = jnp.broadcast_to(row, (16, LANES)).astype(jnp.bfloat16)
    tiled = jnp.concatenate([packed] * (rows // 16), axis=0)
    return jnp.where(mask, tiled, jnp.zeros((rows, LANES), jnp.bfloat16))


def contract_lanes(a, b):
    return lax.dot_general(a, b, (((1,), (1,)), ((), ())), preferred_element_type=jnp.float32)


def gather_owned(row_of, owned_rows, index):
    low = index & (LANES - 1)
    high = index >> 7
    out = [jnp.zeros(index.shape, jnp.float32) for _ in range(3)]
    for h in range(owned_rows):
        hit = high == h
        for r in range(3):
            table = jnp.broadcast_to(row_of(r, h), index.shape)
            out[r] = jnp.where(hit, lane_gather(table, low), out[r])
    return out


def distortion_gradient(corners):
    edge = [[corners[r][m + 1] - corners[r][0] for m in range(3)] for r in range(3)]
    half = [0.5 * (edge[r][0] + edge[r][1] + edge[r][2]) for r in range(3)]
    bent = [[2.0 * edge[r][m] - half[r] for m in range(3)] for r in range(3)]
    norm_sq = None
    for r in range(3):
        for m in range(3):
            term = edge[r][m] * bent[r][m]
            norm_sq = term if norm_sq is None else norm_sq + term
    cof = [[None] * 3 for _ in range(3)]
    for r in range(3):
        r1, r2 = (r + 1) % 3, (r + 2) % 3
        for m in range(3):
            m1, m2 = (m + 1) % 3, (m + 2) % 3
            cof[r][m] = edge[r1][m1] * edge[r2][m2] - edge[r1][m2] * edge[r2][m1]
    root2 = math.sqrt(2.0)
    volume_det = root2 * (edge[0][0] * cof[0][0] + edge[0][1] * cof[0][1] + edge[0][2] * cof[0][2])
    root_term = jnp.sqrt(volume_det * volume_det + 4.0 * delta_reg * delta_reg)
    spread = root_term + jnp.abs(volume_det)
    height = jnp.where(volume_det >= 0, 0.5 * spread, 2.0 * delta_reg * delta_reg / spread)
    outer = (2.0 / 3.0) * jnp.exp((-2.0 / 3.0) * jnp.log(height))
    inner = norm_sq * (root2 / 3.0) / root_term
    gradient = [[None] * 4 for _ in range(3)]
    for r in range(3):
        for m in range(3):
            gradient[r][m + 1] = outer * (bent[r][m] - inner * cof[r][m])
        gradient[r][0] = -(gradient[r][1] + gradient[r][2] + gradient[r][3])
    return gradient


def write_payload(positions_row, owned_rows, send_list_ref, count_ref, out_ref, dom_count):
    dom_here = lax.axis_index("dom")
    slot_count, sub_count, width = send_list_ref.shape
    reach = (slot_count - 1) // 2
    out_ref[...] = jnp.zeros(out_ref.shape, jnp.float32)
    lane = lax.broadcasted_iota(jnp.int32, (1, LANES), 1)
    for k in range(slot_count):
        picked = gather_owned(positions_row, owned_rows, send_list_ref[k])
        target = lax.rem(dom_here + k - reach + dom_count, dom_count) * sub_count
        for t in range(sub_count):
            valid = lane < count_ref[k, t]
            for r in range(3):
                row = jnp.where(valid, picked[r][t : t + 1, :], 0.0)
                out_ref[pl.ds(target + t, 1), 0, r * LANES : (r + 1) * LANES] = row


def send_kernel(positions_ref, send_list_ref, count_ref, out_ref, *, dom_count):
    owned_rows = positions_ref.shape[1] // LANES
    write_payload(
        lambda r, h: positions_ref[r : r + 1, h * LANES : (h + 1) * LANES],
        owned_rows,
        send_list_ref,
        count_ref,
        out_ref,
        dom_count,
    )


def gradient_kernel(
    positions_ref, ghost_ref, pair_nodes_ref, corner_ref, own_ref, back_ref, terms_ref, total_ref, *, dom_count, slot_count
):
    dom_here = lax.axis_index("dom")
    owned_rows = positions_ref.shape[1] // LANES
    sub_count = ghost_ref.shape[0] // dom_count
    reach = (slot_count - 1) // 2
    pair_count = pair_nodes_ref.shape[0]
    high_rows = owned_rows + slot_count * sub_count
    padded = -(-high_rows // 16) * 16

    def ghost_place(k):
        return lax.rem(dom_here - k + reach + dom_count, dom_count) * sub_count

    def local_row(r, h):
        if h < owned_rows:
            return positions_ref[r : r + 1, h * LANES : (h + 1) * LANES]
        k, t = divmod(h - owned_rows, sub_count)
        return ghost_ref[pl.ds(ghost_place(k) + t, 1), 0, r * LANES : (r + 1) * LANES]

    def tets_of_pairs(g, carry):
        index = pair_nodes_ref[pl.ds(pl.multiple_of(g * 8, 8), 8), :]
        nodes = gather_owned(local_row, high_rows, index)
        for q in range(2):
            corners = [[None] * 4 for _ in range(3)]
            for n in range(4):
                place = corner_ref[n, pl.ds(g * 16 + q, 8, stride=2), :] + q * BLOCK_ROWS
                for r in range(3):
                    corners[r][n] = lane_gather(nodes[r], place)
            gradient = distortion_gradient(corners)
            for r in range(3):
                for n in range(4):
                    terms_ref[n, pl.ds(g * 128 + q * 8 + r, 8, stride=16), :] = gradient[r][n]
        return carry

    lax.fori_loop(0, pair_count // 8, tets_of_pairs, 0)
    total_ref[...] = jnp.zeros(total_ref.shape, jnp.float32)
    first_half = lax.broadcasted_iota(jnp.int32, (8, LANES), 1) < BLOCK_ROWS

    def add_pair(p):
        hits = []
        for n in range(4):
            halves = [one_hot(corner_ref[n, pl.ds(2 * p + q, 1), :], BLOCK_ROWS) for q in range(2)]
            hits.append(jnp.concatenate(halves, axis=0))
        start = pl.multiple_of(p * 16, 16)
        terms = []
        for n in range(4):
            terms.append(jnp.concatenate(split_two(terms_ref[n, pl.ds(start, 16), :]), axis=0).astype(jnp.bfloat16))
        terms = jnp.concatenate(terms, axis=1)
        sums = contract_lanes(terms, jnp.concatenate(hits, axis=1))
        sums = sums[:16] + sums[16:]
        node_sums = jnp.where(first_half, sums[:8], sums[8:])
        index = pair_nodes_ref[pl.ds(p, 1), :]
        mask = row_equals(index >> 7, padded)
        rows = []
        for part in split_two(node_sums):
            for r in range(3):
                rows.append(masked_rows(mask, part[r : r + 1, :]))
        return jnp.concatenate(rows, axis=0), one_hot(index & (LANES - 1), LANES)

    def add_pairs(i, carry):
        left, right = zip(*[add_pair(2 * i + j) for j in range(2)])
        total_ref[...] += contract_lanes(jnp.concatenate(left, axis=1), jnp.concatenate(right, axis=1))
        return carry

    lax.fori_loop(0, pair_count // 2, add_pairs, 0)
    back_ref[...] = jnp.zeros(back_ref.shape, jnp.float32)
    for r in range(3):
        summed = total_ref[r * padded : (r + 1) * padded, :] + total_ref[(3 + r) * padded : (4 + r) * padded, :]
        own_ref[r] = summed[:owned_rows]
        for k in range(slot_count):
            target = ghost_place(k)
            for t in range(sub_count):
                h = owned_rows + k * sub_count + t
                back_ref[pl.ds(target + t, 1), 0, r * LANES : (r + 1) * LANES] = summed[h : h + 1]


def moved_positions(positions_ref, mask_ref, own_ref, back_ref, send_list_ref, count_ref, dom_count):
    dom_here = lax.axis_index("dom")
    slot_count, sub_count, width = send_list_ref.shape
    reach = (slot_count - 1) // 2
    owned_rows = own_ref.shape[1]
    lane = lax.broadcasted_iota(jnp.int32, (1, LANES), 1)
    left, right = [], []
    for k in range(slot_count):
        source = lax.rem(dom_here + k - reach + dom_count, dom_count) * sub_count
        for t in range(sub_count):
            index = send_list_ref[k, t : t + 1, :]
            mask = row_equals(index >> 7, owned_rows)
            valid = lane < count_ref[k, t]
            parts = []
            for r in range(3):
                row = back_ref[pl.ds(source + t, 1), 0, r * LANES : (r + 1) * LANES]
                parts.append(split_two(jnp.where(valid, row, 0.0)))
            left.append(jnp.concatenate([masked_rows(mask, parts[r][s]) for s in range(2) for r in range(3)], axis=0))
            right.append(one_hot(index & (LANES - 1), LANES))
    returned = contract_lanes(jnp.concatenate(left, axis=1), jnp.concatenate(right, axis=1))
    free = jnp.where(mask_ref[...] == 0, step_size, 0.0)
    moved = []
    for r in range(3):
        added = returned[r * owned_rows : (r + 1) * owned_rows] + returned[(3 + r) * owned_rows : (4 + r) * owned_rows]
        here = jnp.concatenate(
            [positions_ref[r : r + 1, h * LANES : (h + 1) * LANES] for h in range(owned_rows)], axis=0
        )
        moved.append(here - free * (own_ref[r] + added))
    return moved


def move_kernel(positions_ref, mask_ref, own_ref, back_ref, send_list_ref, count_ref, *out_refs, dom_count):
    moved = moved_positions(positions_ref, mask_ref, own_ref, back_ref, send_list_ref, count_ref, dom_count)
    owned_rows = own_ref.shape[1]
    for r in range(3):
        for h in range(owned_rows):
            out_refs[0][r : r + 1, h * LANES : (h + 1) * LANES] = moved[r][h : h + 1]
    if len(out_refs) > 1:
        write_payload(
            lambda r, h: moved[r][h : h + 1], owned_rows, send_list_ref, count_ref, out_refs[1], dom_count
        )


def per_device(positions, fixed_mask, send_count, send_list, block_nodes, tet_corners):
    node_count = positions.shape[1]
    slot_count, sub_count, width = send_list.shape[2:]
    dom_count = lax.axis_size("dom")
    block_count = block_nodes.shape[1]
    owned_rows = node_count // LANES
    counts = send_count[0, 0]
    lists = send_list[0, 0]
    mask_rows = fixed_mask.reshape(owned_rows, LANES)
    pair_nodes = block_nodes.T.reshape(block_count // 2, LANES)
    corners = tet_corners.reshape(4, block_count, LANES)
    padded = -(-(owned_rows + slot_count * sub_count) // 16) * 16

    vmem = pl.BlockSpec(memory_space=pltpu.VMEM)
    smem = pl.BlockSpec(memory_space=pltpu.SMEM)
    exchange_shape = jax.ShapeDtypeStruct((dom_count * sub_count, 1, 3 * LANES), jnp.float32)
    position_shape = jax.ShapeDtypeStruct(positions.shape, jnp.float32)
    own_shape = jax.ShapeDtypeStruct((3, owned_rows, LANES), jnp.float32)
    params = pltpu.CompilerParams(vmem_limit_bytes=32 * 1024 * 1024)

    send = pl.pallas_call(
        functools.partial(send_kernel, dom_count=dom_count),
        out_shape=exchange_shape,
        in_specs=[vmem, vmem, smem],
        out_specs=vmem,
        compiler_params=params,
        name="send",
    )
    gradient = pl.pallas_call(
        functools.partial(gradient_kernel, dom_count=dom_count, slot_count=slot_count),
        out_shape=(own_shape, exchange_shape),
        in_specs=[vmem] * 4,
        out_specs=(vmem, vmem),
        scratch_shapes=[
            pltpu.VMEM((4, block_count * 8, LANES), jnp.float32),
            pltpu.VMEM((6 * padded, LANES), jnp.float32),
        ],
        compiler_params=params,
        name="gradient",
    )

    def move(last):
        return pl.pallas_call(
            functools.partial(move_kernel, dom_count=dom_count),
            out_shape=(position_shape,) if last else (position_shape, exchange_shape),
            in_specs=[vmem] * 5 + [smem],
            out_specs=(vmem,) if last else (vmem, vmem),
            compiler_params=params,
            name="move_last" if last else "move",
        )

    def exchange(rows):
        return lax.all_to_all(rows, ("dom", "sub"), 0, 0, tiled=True)

    payload = send(positions, lists, counts)
    for step in range(ITERS):
        last = step == ITERS - 1
        ghosts = exchange(payload)
        own, back = gradient(positions, ghosts, pair_nodes, corners)
        returned = exchange(back)
        moved = move(last)(positions, mask_rows, own, returned, lists, counts)
        positions = moved[0]
        if not last:
            payload = moved[1]
    return positions


def solution(mesh):
    return jax.shard_map(
        per_device,
        mesh=mesh,
        in_specs=(
            P(None, ("dom", "sub")),
            P(("dom", "sub")),
            P("dom", "sub", None, None),
            P("dom", "sub", None, None, None),
            P(None, ("dom", "sub")),
            P(None, ("dom", "sub")),
        ),
        out_specs=P(None, ("dom", "sub")),
        check_vma=False,
    )
```

time: 571 us -> 78.7 us (0.14)
  other arithmetic: 226 us -> 0 us
  local copies, waits for them, and re-layouts: 203 us -> 3.19 us
  matrix products: 67.2 us -> 0 us
  Pallas kernels: 0 us -> 34.3 us
  waiting for transfers between devices: 26.4 us -> 6.37 us
  starting transfers between devices: 23.8 us -> 7.3 us
  blocking collectives: 18.3 us -> 27.1 us
    scatter-add x4 -> x0, other arithmetic: 119 us -> none  [the longest x2 90 us: tet_energy(): block_coords = local_nodes[:, block_nodes.T]]
    dynamic_update_slice x80 -> x0, local copies, waits for them, and re-layouts: 74.3 us -> none  [tet_energy(): return jnp.sum(lax.map(group_energy, (block_coords, corner_rows)))]
    gather x12 -> x0, local copies, waits for them, and re-layouts: 73.2 us -> none  [the longest x4 61.4 us: tet_energy(): block_coords = local_nodes[:, block_nodes.T]]
    dot_general x32 -> x0, matrix products: 67.2 us -> none  [group_energy(): jnp.einsum('rgm,ngim->rngi', coords, incidence, precision=lax.Precision.H...]
    convert_element_type x16 -> x0, other arithmetic: 48.3 us -> none  [group_energy(): (rows[:, :, :, None] == column_ids[None, None, None, :]).astype(jnp.float32)]
    pallas_call x0 -> x5, Pallas kernels: none -> 34.3 us  [the longest x2 29.8 us: per_device(): own, back = gradient(positions, ghosts, pair_nodes, corners)]
    dynamic_update_slice x64 -> x0, other arithmetic: 26.1 us -> none  [tet_energy(): return jnp.sum(lax.map(group_energy, (block_coords, corner_rows)))]
    neg x64 -> x0, other arithmetic: 25.2 us -> none  [distortion_sum(): corners[r, m + 1] - corners[r, 0]]
  transfers between devices with their start and end apart: 6 -> 1, of which waited for: 6 -> 1; matrix products, arithmetic and copies ran while one was open for 1% -> 1% of each run, Pallas kernels for 0% -> 0%
where the time goes in v1:
time: 78.7 us; the launch traced here: 78.3 us
  Pallas kernels  34.3 us (44%)
  blocking collectives  27.1 us (34%)
  starting transfers between devices  7.3 us (9%)
  waiting for transfers between devices  6.37 us (8%)
  local copies, waits for them, and re-layouts  3.19 us (4%)
    pallas_call x2, Pallas kernels, per_device(): own, back = gradient(positions, ghosts, pair_nodes, corners)  29.8 us
    all_to_all x3, blocking collectives, exchange(): return lax.all_to_all(rows, ('dom', 'sub'), 0, 0, tiled=True)  27.1 us
    all_to_all x1, starting transfers between devices, exchange(): return lax.all_to_all(rows, ('dom', 'sub'), 0, 0, tiled=True)  7.3 us
    all_to_all x1, waiting for transfers between devices, exchange(): return lax.all_to_all(rows, ('dom', 'sub'), 0, 0, tiled=True)  6.37 us
    pallas_call x2, Pallas kernels, per_device(): moved = move(last)(positions, mask_rows, own, returned, lists, counts)  2.92 us
  transfers between devices with their start and end apart: 1, of which 1 were waited for; matrix products, arithmetic and copies ran while one was open for 1% of the time, Pallas kernels for 0%

profile of v1, /device:TPU:0, one launch (start us, length us, event | category | flops | bytes accessed | tf_op | source)
XLA Modules:
  0.0 78.3 jit_solution(11893430433189064571)
XLA Ops:
  0.0 0.8 copy.11.count_ref
  0.8 0.0 copy-start
  0.8 0.8 copy-done
  1.5 0.0 copy-start.2
  1.5 0.7 copy-done.2
  2.2 0.0 copy-start.5
  2.2 1.6 %send.1 = f32[32,1,384]{2,1,0:T(1,128)} custom-call(f32[3,2048]{1,0:T(4,128)S(1)} %copy-done, s32[5,4,128]{2,1,0:T(4,128)S(1)} %bitcast.10, s32[5,4]{1,0:T(8,128)S(1)} %copy.11.count_ref), custom_call_target="tpu_custom_call" | custom-call | tf_op jit(solution)/shard_map/send/pallas_call | solution.py:311
  3.8 7.3 %all-to-all-start = ((f32[32,1,384]{2,1,0:T(1,128)}), f32[32,1,384]{2,1,0:T(1,128)S(1)}, u32[]{:S(2)}, u32[]{:S(2)}) async-start(f32[32,1,384]{2,1,0:T(1,128)} %send.1), calls=%async_computation | async-start | bytes 98304 | tf_op jit(solution)/shard_map/all_to_all | solution.py:309
  11.1 0.8 %copy.12 = s32[128,64]{1,0:T(8,128)S(1)} copy(s32[128,64]{0,1:T(8,128)} %bitcast.16) | data formatting | bytes 65536 | tf_op jit(solution)/shard_map/transpose | solution.py:266
  11.9 0.1 reshape.10.pair_nodes_ref
  12.0 0.0 copy-done.5
  12.0 0.0 copy-start.1
  12.1 6.4 %all-to-all-done.ghost_ref = f32[32,1,384]{2,1,0:T(1,128)S(1)} async-done(((f32[32,1,384]{2,1,0:T(1,128)}), f32[32,1,384]{2,1,0:T(1,128)S(1)}, u32[]{:S(2)}, u32[]{:S(2)}) %all-to-all-start) | async-done | bytes 49184 | tf_op jit(solution)/shard_map/all_to_all | solution.py:309
  18.4 0.0 copy-done.1
  18.4 14.9 %gradient.2 = (f32[3,16,128]{2,1,0:T(8,128)S(1)}, f32[32,1,384]{2,1,0:T(1,128)S(1)}) custom-call(f32[3,2048]{1,0:T(4,128)S(1)} %copy-done.1, f32[32,1,384]{2,1,0:T(1,128)S(1)} %all-to-all-done.ghost_ref, s32[64,128]{1,0:T(8,128)S(1)} %reshape.10.pair_nodes_ref, s32[4,128,128]{2,1,0:T(8,128)S(1)} %bitcast.8), custom_call_target="tpu_custom_call" | custom-call | tf_op jit(solution)/shard_map/gradient/pallas_call | solution.py:315
  33.3 0.0 copy-start.3
  33.3 0.0 copy-start.4
  33.4 9.0 %all_to_all.20.back_ref = f32[32,1,384]{2,1,0:T(1,128)S(1)} all-to-all(f32[32,1,384]{2,1,0:T(1,128)S(1)} %get-tuple-element.12), channel_id=1, replica_groups=mesh['dom'=8,'sub'=4] {'dom','sub'}, dimensions={0} | all-to-all | bytes 98304 | tf_op jit(solution)/shard_map/all_to_all | solution.py:309
  42.4 0.0 copy-done.3
  42.4 0.0 copy-done.4
  42.4 1.3 %move.1 = (f32[3,2048]{1,0:T(4,128)S(1)}, f32[32,1,384]{2,1,0:T(1,128)S(1)}) custom-call(f32[3,2048]{1,0:T(4,128)S(1)} %copy-done.1, s32[16,128]{1,0:T(8,128)S(1)} %bitcast.13, f32[3,16,128]{2,1,0:T(8,128)S(1)} %get-tuple-element.11.own_ref, f32[32,1,384]{2,1,0:T(1,128)S(1)} %all_to_all.20.back_ref, s32[5,4,128]{2,1,0:T(4,128)S(1)} %bitcast.11, ...), custom_call_target="tpu_custom_call" | custom-call | tf_op jit(solution)/shard_map/move/pallas_call | solution.py:317
  43.7 9.0 %all_to_all.21.ghost_ref = f32[32,1,384]{2,1,0:T(1,128)S(1)} all-to-all(f32[32,1,384]{2,1,0:T(1,128)S(1)} %get-tuple-element.14), channel_id=1, replica_groups=mesh['dom'=8,'sub'=4] {'dom','sub'}, dimensions={0} | all-to-all | bytes 98304 | tf_op jit(solution)/shard_map/all_to_all | solution.py:309
  52.8 14.9 %gradient.3 = (f32[3,16,128]{2,1,0:T(8,128)S(1)}, f32[32,1,384]{2,1,0:T(1,128)S(1)}) custom-call(f32[3,2048]{1,0:T(4,128)S(1)} %get-tuple-element.13.positions_ref, f32[32,1,384]{2,1,0:T(1,128)S(1)} %all_to_all.21.ghost_ref, s32[64,128]{1,0:T(8,128)S(1)} %reshape.10.pair_nodes_ref, s32[4,128,128]{2,1,0:T(8,128)S(1)} %bitcast.9), custom_call_target="tpu_custom_call" | custom-call | tf_op jit(solution)/shard_map/gradient/pallas_call | solution.py:315
  67.7 9.0 %all_to_all.22.back_ref = f32[32,1,384]{2,1,0:T(1,128)S(1)} all-to-all(f32[32,1,384]{2,1,0:T(1,128)S(1)} %get-tuple-element.16), channel_id=1, replica_groups=mesh['dom'=8,'sub'=4] {'dom','sub'}, dimensions={0} | all-to-all | bytes 98304 | tf_op jit(solution)/shard_map/all_to_all | solution.py:309
  76.7 1.6 %move_last.1 = f32[3,2048]{1,0:T(4,128)} custom-call(f32[3,2048]{1,0:T(4,128)S(1)} %get-tuple-element.13.positions_ref, s32[16,128]{1,0:T(8,128)S(1)} %bitcast.14, f32[3,16,128]{2,1,0:T(8,128)S(1)} %get-tuple-element.15.own_ref, f32[32,1,384]{2,1,0:T(1,128)S(1)} %all_to_all.22.back_ref, s32[5,4,128]{2,1,0:T(4,128)S(1)} %bitcast.12, s32[5,4]{1,0:T(8,128)S(1)} %copy.11.count_ref), custom_call_target="tpu_custom_call" | custom-call | tf_op jit(solution)/shard_map/move_last/pallas_call | solution.py:317
  (1 shorter events, 0.0 us)
Async XLA Ops:
  0.8 0.8 copy-start
  1.5 0.7 copy-start.2
  2.2 9.8 %copy-start.5 = (s32[4,16384]{1,0:T(4,128)S(1)}, s32[4,16384]{1,0:T(4,128)}, u32[]{:S(2)}) copy-start(s32[4,16384]{1,0:T(4,128)} %param.11) | copy-start | bytes 786436
  3.8 14.6 %all-to-all-start = ((f32[32,1,384]{2,1,0:T(1,128)}), f32[32,1,384]{2,1,0:T(1,128)S(1)}, u32[]{:S(2)}, u32[]{:S(2)}) async-start(f32[32,1,384]{2,1,0:T(1,128)} %send.1), calls=%async_computation | async-start | bytes 98304 | tf_op jit(solution)/shard_map/all_to_all | solution.py:309
  12.0 6.4 %copy-start.1 = (f32[3,2048]{1,0:T(4,128)S(1)}, f32[3,2048]{1,0:T(4,128)}, u32[]{:S(2)}) copy-start(f32[3,2048]{1,0:T(4,128)} %positions_ref.5) | copy-start | bytes 73732
  33.3 9.1 %copy-start.3 = (s32[1,1,5,4,128]{4,3,2,1,0:T(4,128)S(1)}, s32[1,1,5,4,128]{4,3,2,1,0:T(4,128)}, u32[]{:S(2)}) copy-start(s32[1,1,5,4,128]{4,3,2,1,0:T(4,128)} %param.9) | copy-start | bytes 30724
  33.3 9.0 %copy-start.4 = (s32[2048]{0:T(1024)S(1)}, s32[2048]{0:T(1024)}, u32[]{:S(2)}) copy-start(s32[2048]{0:T(1024)} %param.7) | copy-start | bytes 24580

commit v2 on v1

--- a/solution.py
+++ b/solution.py
@@ -39,7 +39,7 @@
 
 
 def row_equals(ids_row, rows):
-    packed = jnp.broadcast_to(ids_row.astype(jnp.float32), (16, LANES)).astype(jnp.bfloat16)
+    packed = jnp.broadcast_to(ids_row, (16, LANES)).astype(jnp.bfloat16)
     return jnp.concatenate([packed] * (rows // 16), axis=0) == row_iota(rows)
 
 
@@ -135,7 +135,7 @@
 
 
 def gradient_kernel(
-    positions_ref, ghost_ref, pair_nodes_ref, corner_ref, own_ref, back_ref, terms_ref, total_ref, *, dom_count, slot_count
+    positions_ref, ghost_ref, pair_nodes_ref, corner_ref, own_ref, back_ref, place_ref, terms_ref, node_ref, total_ref, *, dom_count, slot_count
 ):
     dom_here = lax.axis_index("dom")
     owned_rows = positions_ref.shape[1] // LANES
@@ -154,52 +154,51 @@
         k, t = divmod(h - owned_rows, sub_count)
         return ghost_ref[pl.ds(ghost_place(k) + t, 1), 0, r * LANES : (r + 1) * LANES]
 
-    def tets_of_pairs(g, carry):
-        index = pair_nodes_ref[pl.ds(pl.multiple_of(g * 8, 8), 8), :]
+    def tets_of_pairs(g):
+        index = pair_nodes_ref[pl.ds(g * 8, 8), :]
         nodes = gather_owned(local_row, high_rows, index)
         for q in range(2):
             corners = [[None] * 4 for _ in range(3)]
             for n in range(4):
-                place = corner_ref[n, pl.ds(g * 16 + q, 8, stride=2), :] + q * BLOCK_ROWS
+                place = corner_ref[n, pl.ds(g * 16 + q, 8, stride=2), :]
+                place_ref[n, pl.ds(g * 16 + q, 8, stride=2), :] = place.astype(jnp.float32)
+                place = place + q * BLOCK_ROWS
                 for r in range(3):
                     corners[r][n] = lane_gather(nodes[r], place)
             gradient = distortion_gradient(corners)
             for r in range(3):
                 for n in range(4):
-                    terms_ref[n, pl.ds(g * 128 + q * 8 + r, 8, stride=16), :] = gradient[r][n]
-        return carry
-
-    lax.fori_loop(0, pair_count // 8, tets_of_pairs, 0)
-    total_ref[...] = jnp.zeros(total_ref.shape, jnp.float32)
+                    for s, part in enumerate(split_two(gradient[r][n])):
+                        terms_ref[n, pl.ds(g * 128 + q * 8 + s * 4 + r, 8, stride=16), :] = part
+
+    for g in range(pair_count // 8):
+        tets_of_pairs(g)
     first_half = lax.broadcasted_iota(jnp.int32, (8, LANES), 1) < BLOCK_ROWS
 
-    def add_pair(p):
+    def add_tets(p):
         hits = []
         for n in range(4):
-            halves = [one_hot(corner_ref[n, pl.ds(2 * p + q, 1), :], BLOCK_ROWS) for q in range(2)]
+            halves = [one_hot(place_ref[n, pl.ds(2 * p + q, 1), :], BLOCK_ROWS) for q in range(2)]
             hits.append(jnp.concatenate(halves, axis=0))
-        start = pl.multiple_of(p * 16, 16)
-        terms = []
-        for n in range(4):
-            terms.append(jnp.concatenate(split_two(terms_ref[n, pl.ds(start, 16), :]), axis=0).astype(jnp.bfloat16))
-        terms = jnp.concatenate(terms, axis=1)
-        sums = contract_lanes(terms, jnp.concatenate(hits, axis=1))
-        sums = sums[:16] + sums[16:]
-        node_sums = jnp.where(first_half, sums[:8], sums[8:])
+        terms = [terms_ref[n, pl.ds(p * 16, 16), :].astype(jnp.bfloat16) for n in range(4)]
+        sums = contract_lanes(jnp.concatenate(terms, axis=1), jnp.concatenate(hits, axis=1))
+        sums = jnp.where(first_half, sums[:8], sums[8:])
+        node_ref[pl.ds(p * 8, 8), :] = sums + pltpu.roll(sums, 4, 0)
+
+    for p in range(pair_count):
+        add_tets(p)
+
+    def node_rows(p):
         index = pair_nodes_ref[pl.ds(p, 1), :]
-        mask = row_equals(index >> 7, padded)
+        mask = row_equals((index >> 7).astype(jnp.float32), padded)
         rows = []
-        for part in split_two(node_sums):
+        for part in split_two(node_ref[pl.ds(p * 8, 8), :]):
             for r in range(3):
                 rows.append(masked_rows(mask, part[r : r + 1, :]))
-        return jnp.concatenate(rows, axis=0), one_hot(index & (LANES - 1), LANES)
-
-    def add_pairs(i, carry):
-        left, right = zip(*[add_pair(2 * i + j) for j in range(2)])
-        total_ref[...] += contract_lanes(jnp.concatenate(left, axis=1), jnp.concatenate(right, axis=1))
-        return carry
-
-    lax.fori_loop(0, pair_count // 2, add_pairs, 0)
+        return jnp.concatenate(rows, axis=0), one_hot((index & (LANES - 1)).astype(jnp.float32), LANES)
+
+    left, right = zip(*[node_rows(p) for p in range(pair_count)])
+    total_ref[...] = contract_lanes(jnp.concatenate(left, axis=1), jnp.concatenate(right, axis=1))
     back_ref[...] = jnp.zeros(back_ref.shape, jnp.float32)
     for r in range(3):
         summed = total_ref[r * padded : (r + 1) * padded, :] + total_ref[(3 + r) * padded : (4 + r) * padded, :]
@@ -222,14 +221,14 @@
         source = lax.rem(dom_here + k - reach + dom_count, dom_count) * sub_count
         for t in range(sub_count):
             index = send_list_ref[k, t : t + 1, :]
-            mask = row_equals(index >> 7, owned_rows)
+            mask = row_equals((index >> 7).astype(jnp.float32), owned_rows)
             valid = lane < count_ref[k, t]
             parts = []
             for r in range(3):
                 row = back_ref[pl.ds(source + t, 1), 0, r * LANES : (r + 1) * LANES]
                 parts.append(split_two(jnp.where(valid, row, 0.0)))
             left.append(jnp.concatenate([masked_rows(mask, parts[r][s]) for s in range(2) for r in range(3)], axis=0))
-            right.append(one_hot(index & (LANES - 1), LANES))
+            right.append(one_hot((index & (LANES - 1)).astype(jnp.float32), LANES))
     returned = contract_lanes(jnp.concatenate(left, axis=1), jnp.concatenate(right, axis=1))
     free = jnp.where(mask_ref[...] == 0, step_size, 0.0)
     moved = []
@@ -288,7 +287,9 @@
         in_specs=[vmem] * 4,
         out_specs=(vmem, vmem),
         scratch_shapes=[
+            pltpu.VMEM((4, block_count, LANES), jnp.float32),
             pltpu.VMEM((4, block_count * 8, LANES), jnp.float32),
+            pltpu.VMEM((block_count * 4, LANES), jnp.float32),
             pltpu.VMEM((6 * padded, LANES), jnp.float32),
         ],
         compiler_params=params,

time: 78.7 us -> 57.4 us (0.73)
  Pallas kernels: 34.3 us -> 12.9 us
    pallas_call x2, Pallas kernels: 29.8 us -> 8.45 us  [per_device(): own, back = gradient(positions, ghosts, pair_nodes, corners)]
  transfers between devices with their start and end apart: 1 -> 1, of which waited for: 1 -> 1; matrix products, arithmetic and copies ran while one was open for 1% -> 2% of each run, Pallas kernels for 0% -> 0%
where the time goes in v2:
time: 57.4 us; the launch traced here: 56.9 us
  blocking collectives  27.1 us (47%)
  Pallas kernels  12.9 us (22%)
  starting transfers between devices  7.3 us (13%)
  waiting for transfers between devices  6.37 us (11%)
  local copies, waits for them, and re-layouts  3.19 us (6%)
    all_to_all x3, blocking collectives, exchange(): return lax.all_to_all(rows, ('dom', 'sub'), 0, 0, tiled=True)  27.1 us
    pallas_call x2, Pallas kernels, per_device(): own, back = gradient(positions, ghosts, pair_nodes, corners)  8.45 us
    all_to_all x1, starting transfers between devices, exchange(): return lax.all_to_all(rows, ('dom', 'sub'), 0, 0, tiled=True)  7.3 us
    all_to_all x1, waiting for transfers between devices, exchange(): return lax.all_to_all(rows, ('dom', 'sub'), 0, 0, tiled=True)  6.37 us
    pallas_call x2, Pallas kernels, per_device(): moved = move(last)(positions, mask_rows, own, returned, lists, counts)  2.92 us
    pallas_call x1, Pallas kernels, per_device(): payload = send(positions, lists, counts)  1.56 us
    unnamed x13, local copies, waits for them, and re-layouts  1.5 us
  transfers between devices with their start and end apart: 1, of which 1 were waited for; matrix products, arithmetic and copies ran while one was open for 2% of the time, Pallas kernels for 0%

profile of v2, /device:TPU:0, one launch (start us, length us, event | category | flops | bytes accessed | tf_op | source)
XLA Modules:
  0.0 56.9 jit_solution(9356930357609008512)
XLA Ops:
  0.0 0.8 %copy.11.count_ref = s32[5,4]{1,0:T(8,128)S(1)} copy(s32[5,4]{0,1:T(4,128)} %bitcast.17) | data formatting | bytes 160 | tf_op jit(solution)/shard_map/squeeze | solution.py:262
  0.8 0.0 copy-start
  0.8 0.8 %copy-done = f32[3,2048]{1,0:T(4,128)S(1)} copy-done((f32[3,2048]{1,0:T(4,128)S(1)}, f32[3,2048]{1,0:T(4,128)}, u32[]{:S(2)}) %copy-start) | copy-done | bytes 24600
  1.5 0.0 copy-start.2
  1.5 0.7 %copy-done.2 = s32[1,1,5,4,128]{4,3,2,1,0:T(4,128)S(1)} copy-done((s32[1,1,5,4,128]{4,3,2,1,0:T(4,128)S(1)}, s32[1,1,5,4,128]{4,3,2,1,0:T(4,128)}, u32[]{:S(2)}) %copy-start.2) | copy-done | bytes 10264
  2.2 0.0 copy-start.5
  2.2 1.6 %send.1 = f32[32,1,384]{2,1,0:T(1,128)} custom-call(f32[3,2048]{1,0:T(4,128)S(1)} %copy-done, s32[5,4,128]{2,1,0:T(4,128)S(1)} %bitcast.10, s32[5,4]{1,0:T(8,128)S(1)} %copy.11.count_ref), custom_call_target="tpu_custom_call" | custom-call | tf_op jit(solution)/shard_map/send/pallas_call | solution.py:312
  3.8 7.3 %all-to-all-start = ((f32[32,1,384]{2,1,0:T(1,128)}), f32[32,1,384]{2,1,0:T(1,128)S(1)}, u32[]{:S(2)}, u32[]{:S(2)}) async-start(f32[32,1,384]{2,1,0:T(1,128)} %send.1), calls=%async_computation | async-start | bytes 98304 | tf_op jit(solution)/shard_map/all_to_all | solution.py:310
  11.1 0.8 %copy.12 = s32[128,64]{1,0:T(8,128)S(1)} copy(s32[128,64]{0,1:T(8,128)} %bitcast.16) | data formatting | bytes 65536 | tf_op jit(solution)/shard_map/transpose | solution.py:265
  11.9 0.1 reshape.10.pair_nodes_ref
  12.0 0.0 copy-done.5
  12.0 0.0 copy-start.1
  12.1 6.4 %all-to-all-done.ghost_ref = f32[32,1,384]{2,1,0:T(1,128)S(1)} async-done(((f32[32,1,384]{2,1,0:T(1,128)}), f32[32,1,384]{2,1,0:T(1,128)S(1)}, u32[]{:S(2)}, u32[]{:S(2)}) %all-to-all-start) | async-done | bytes 49184 | tf_op jit(solution)/shard_map/all_to_all | solution.py:310
  18.4 0.0 copy-done.1
  18.4 4.2 %gradient.2 = (f32[3,16,128]{2,1,0:T(8,128)S(1)}, f32[32,1,384]{2,1,0:T(1,128)S(1)}) custom-call(f32[3,2048]{1,0:T(4,128)S(1)} %copy-done.1, f32[32,1,384]{2,1,0:T(1,128)S(1)} %all-to-all-done.ghost_ref, s32[64,128]{1,0:T(8,128)S(1)} %reshape.10.pair_nodes_ref, s32[4,128,128]{2,1,0:T(8,128)S(1)} %bitcast.8), custom_call_target="tpu_custom_call" | custom-call | tf_op jit(solution)/shard_map/gradient/pallas_call | solution.py:316
  22.7 0.0 copy-start.3
  22.7 0.0 copy-start.4
  22.7 9.0 %all_to_all.20.back_ref = f32[32,1,384]{2,1,0:T(1,128)S(1)} all-to-all(f32[32,1,384]{2,1,0:T(1,128)S(1)} %get-tuple-element.12), channel_id=1, replica_groups=mesh['dom'=8,'sub'=4] {'dom','sub'}, dimensions={0} | all-to-all | bytes 98304 | tf_op jit(solution)/shard_map/all_to_all | solution.py:310
  31.7 0.0 copy-done.3
  31.7 0.0 copy-done.4
  31.7 1.3 %move.1 = (f32[3,2048]{1,0:T(4,128)S(1)}, f32[32,1,384]{2,1,0:T(1,128)S(1)}) custom-call(f32[3,2048]{1,0:T(4,128)S(1)} %copy-done.1, s32[16,128]{1,0:T(8,128)S(1)} %bitcast.13, f32[3,16,128]{2,1,0:T(8,128)S(1)} %get-tuple-element.11.own_ref, f32[32,1,384]{2,1,0:T(1,128)S(1)} %all_to_all.20.back_ref, s32[5,4,128]{2,1,0:T(4,128)S(1)} %bitcast.11, ...), custom_call_target="tpu_custom_call" | custom-call | tf_op jit(solution)/shard_map/move/pallas_call | solution.py:318
  33.1 9.0 %all_to_all.21.ghost_ref = f32[32,1,384]{2,1,0:T(1,128)S(1)} all-to-all(f32[32,1,384]{2,1,0:T(1,128)S(1)} %get-tuple-element.14), channel_id=1, replica_groups=mesh['dom'=8,'sub'=4] {'dom','sub'}, dimensions={0} | all-to-all | bytes 98304 | tf_op jit(solution)/shard_map/all_to_all | solution.py:310
  42.1 4.2 %gradient.3 = (f32[3,16,128]{2,1,0:T(8,128)S(1)}, f32[32,1,384]{2,1,0:T(1,128)S(1)}) custom-call(f32[3,2048]{1,0:T(4,128)S(1)} %get-tuple-element.13.positions_ref, f32[32,1,384]{2,1,0:T(1,128)S(1)} %all_to_all.21.ghost_ref, s32[64,128]{1,0:T(8,128)S(1)} %reshape.10.pair_nodes_ref, s32[4,128,128]{2,1,0:T(8,128)S(1)} %bitcast.9), custom_call_target="tpu_custom_call" | custom-call | tf_op jit(solution)/shard_map/gradient/pallas_call | solution.py:316
  46.3 9.0 %all_to_all.22.back_ref = f32[32,1,384]{2,1,0:T(1,128)S(1)} all-to-all(f32[32,1,384]{2,1,0:T(1,128)S(1)} %get-tuple-element.16), channel_id=1, replica_groups=mesh['dom'=8,'sub'=4] {'dom','sub'}, dimensions={0} | all-to-all | bytes 98304 | tf_op jit(solution)/shard_map/all_to_all | solution.py:310
  55.4 1.6 %move_last.1 = f32[3,2048]{1,0:T(4,128)} custom-call(f32[3,2048]{1,0:T(4,128)S(1)} %get-tuple-element.13.positions_ref, s32[16,128]{1,0:T(8,128)S(1)} %bitcast.14, f32[3,16,128]{2,1,0:T(8,128)S(1)} %get-tuple-element.15.own_ref, f32[32,1,384]{2,1,0:T(1,128)S(1)} %all_to_all.22.back_ref, s32[5,4,128]{2,1,0:T(4,128)S(1)} %bitcast.12, s32[5,4]{1,0:T(8,128)S(1)} %copy.11.count_ref), custom_call_target="tpu_custom_call" | custom-call | tf_op jit(solution)/shard_map/move_last/pallas_call | solution.py:318
  (1 shorter events, 0.0 us)
Async XLA Ops:
  0.8 0.8 %copy-start = (f32[3,2048]{1,0:T(4,128)S(1)}, f32[3,2048]{1,0:T(4,128)}, u32[]{:S(2)}) copy-start(f32[3,2048]{1,0:T(4,128)} %positions_ref.5) | copy-start | bytes 73732
  1.5 0.7 %copy-start.2 = (s32[1,1,5,4,128]{4,3,2,1,0:T(4,128)S(1)}, s32[1,1,5,4,128]{4,3,2,1,0:T(4,128)}, u32[]{:S(2)}) copy-start(s32[1,1,5,4,128]{4,3,2,1,0:T(4,128)} %param.9) | copy-start | bytes 30724
  2.2 9.8 %copy-start.5 = (s32[4,16384]{1,0:T(4,128)S(1)}, s32[4,16384]{1,0:T(4,128)}, u32[]{:S(2)}) copy-start(s32[4,16384]{1,0:T(4,128)} %param.11) | copy-start | bytes 786436
  3.8 14.6 %all-to-all-start = ((f32[32,1,384]{2,1,0:T(1,128)}), f32[32,1,384]{2,1,0:T(1,128)S(1)}, u32[]{:S(2)}, u32[]{:S(2)}) async-start(f32[32,1,384]{2,1,0:T(1,128)} %send.1), calls=%async_computation | async-start | bytes 98304 | tf_op jit(solution)/shard_map/all_to_all | solution.py:310
  12.0 6.4 %copy-start.1 = (f32[3,2048]{1,0:T(4,128)S(1)}, f32[3,2048]{1,0:T(4,128)}, u32[]{:S(2)}) copy-start(f32[3,2048]{1,0:T(4,128)} %positions_ref.5) | copy-start | bytes 73732
  22.7 9.1 %copy-start.3 = (s32[1,1,5,4,128]{4,3,2,1,0:T(4,128)S(1)}, s32[1,1,5,4,128]{4,3,2,1,0:T(4,128)}, u32[]{:S(2)}) copy-start(s32[1,1,5,4,128]{4,3,2,1,0:T(4,128)} %param.9) | copy-start | bytes 30724
  22.7 9.0 %copy-start.4 = (s32[2048]{0:T(1024)S(1)}, s32[2048]{0:T(1024)}, u32[]{:S(2)}) copy-start(s32[2048]{0:T(1024)} %param.7) | copy-start | bytes 24580

commit v3 on v2

v3 whole, which is shorter than its diff:
```python
import functools
import math

import jax
import jax.numpy as jnp
from jax import lax
from jax.experimental import pallas as pl
from jax.experimental.pallas import tpu as pltpu
from jax.sharding import PartitionSpec as P

ITERS = 2
LANES = 128
BLOCK_ROWS = 64

delta_reg = 2.0
step_size = 0.01

LANE_GATHER = lax.GatherDimensionNumbers(
    offset_dims=(),
    collapsed_slice_dims=(1,),
    start_index_map=(1,),
    operand_batching_dims=(0,),
    start_indices_batching_dims=(0,),
)


def lane_gather(table, index):
    return lax.gather(
        table,
        index[:, :, None],
        LANE_GATHER,
        slice_sizes=(1, 1),
        mode=lax.GatherScatterMode.PROMISE_IN_BOUNDS,
    )


def row_iota(rows):
    return lax.broadcasted_iota(jnp.int32, (rows, LANES), 0).astype(jnp.float32).astype(jnp.bfloat16)


def row_equals(ids_row, rows):
    packed = jnp.broadcast_to(ids_row, (16, LANES)).astype(jnp.bfloat16)
    return jnp.concatenate([packed] * (rows // 16), axis=0) == row_iota(rows)


def one_hot(ids_row, rows):
    mask = row_equals(ids_row, rows)
    return jnp.where(mask, jnp.ones((rows, LANES), jnp.bfloat16), jnp.zeros((rows, LANES), jnp.bfloat16))


def split_two(values):
    upper = values.astype(jnp.bfloat16).astype(jnp.float32)
    return upper, values - upper


def masked_rows(mask, row):
    rows = mask.shape[0]
    packed = jnp.broadcast_to(row, (16, LANES)).astype(jnp.bfloat16)
    tiled = jnp.concatenate([packed] * (rows // 16), axis=0)
    return jnp.where(mask, tiled, jnp.zeros((rows, LANES), jnp.bfloat16))


def contract_lanes(a, b):
    return lax.dot_general(a, b, (((1,), (1,)), ((), ())), preferred_element_type=jnp.float32)


def gather_rows(row_of, first, last, index, out):
    low = index & (LANES - 1)
    high = index >> 7
    out = list(out)
    for h in range(first, last):
        hit = high == h
        for r in range(3):
            table = jnp.broadcast_to(row_of(r, h), index.shape)
            out[r] = jnp.where(hit, lane_gather(table, low), out[r])
    return out


def distortion_gradient(corners):
    edge = [[corners[r][m + 1] - corners[r][0] for m in range(3)] for r in range(3)]
    half = [0.5 * (edge[r][0] + edge[r][1] + edge[r][2]) for r in range(3)]
    bent = [[2.0 * edge[r][m] - half[r] for m in range(3)] for r in range(3)]
    norm_sq = None
    for r in range(3):
        for m in range(3):
            term = edge[r][m] * bent[r][m]
            norm_sq = term if norm_sq is None else norm_sq + term
    cof = [[None] * 3 for _ in range(3)]
    for r in range(3):
        r1, r2 = (r + 1) % 3, (r + 2) % 3
        for m in range(3):
            m1, m2 = (m + 1) % 3, (m + 2) % 3
            cof[r][m] = edge[r1][m1] * edge[r2][m2] - edge[r1][m2] * edge[r2][m1]
    root2 = math.sqrt(2.0)
    volume_det = root2 * (edge[0][0] * cof[0][0] + edge[0][1] * cof[0][1] + edge[0][2] * cof[0][2])
    root_term = jnp.sqrt(volume_det * volume_det + 4.0 * delta_reg * delta_reg)
    spread = root_term + jnp.abs(volume_det)
    height = jnp.where(volume_det >= 0, 0.5 * spread, 2.0 * delta_reg * delta_reg / spread)
    outer = (2.0 / 3.0) * jnp.exp((-2.0 / 3.0) * jnp.log(height))
    inner = norm_sq * (root2 / 3.0) / root_term
    gradient = [[None] * 4 for _ in range(3)]
    for r in range(3):
        for m in range(3):
            gradient[r][m + 1] = outer * (bent[r][m] - inner * cof[r][m])
        gradient[r][0] = -(gradient[r][1] + gradient[r][2] + gradient[r][3])
    return gradient


def position_row(positions_ref):
    return lambda r, h: positions_ref[r : r + 1, h * LANES : (h + 1) * LANES]


def write_payload(row_of, owned_rows, list_ref, valid_ref, out_ref, dom_count):
    dom_here = lax.axis_index("dom")
    slot_count, sub_count, width = list_ref.shape
    reach = (slot_count - 1) // 2
    out_ref[...] = jnp.zeros(out_ref.shape, jnp.float32)
    group = max(1, 8 // sub_count)
    for first in range(0, slot_count, group):
        slots = range(first, min(first + group, slot_count))
        index = jnp.concatenate([list_ref[k] for k in slots], axis=0)
        valid = jnp.concatenate([valid_ref[k] for k in slots], axis=0)
        zeros = [jnp.zeros(index.shape, jnp.float32)] * 3
        picked = [x * valid for x in gather_rows(row_of, 0, owned_rows, index, zeros)]
        for i, k in enumerate(slots):
            target = lax.rem(dom_here + k - reach + dom_count, dom_count) * sub_count
            for t in range(sub_count):
                for r in range(3):
                    row = picked[r][i * sub_count + t : i * sub_count + t + 1, :]
                    out_ref[pl.ds(target + t, 1), 0, r * LANES : (r + 1) * LANES] = row


def send_kernel(positions_hbm, list_hbm, count_hbm, out_ref, valid_ref, positions_ref, list_ref, count_ref, sems, *, dom_count):
    copies = [
        pltpu.make_async_copy(source, target, sems.at[i])
        for i, (source, target) in enumerate(
            [(positions_hbm, positions_ref), (list_hbm, list_ref), (count_hbm, count_ref)]
        )
    ]
    for copy in copies:
        copy.start()
    for copy in copies:
        copy.wait()
    slot_count, sub_count, width = list_ref.shape
    lane = lax.broadcasted_iota(jnp.int32, (sub_count, LANES), 1)
    for k in range(slot_count):
        counts = jnp.broadcast_to(count_ref[:, k : k + 1], (sub_count, LANES))
        valid_ref[k] = jnp.where(lane < counts, 1.0, 0.0)
    write_payload(
        position_row(positions_ref), positions_ref.shape[1] // LANES, list_ref, valid_ref, out_ref, dom_count
    )


def owned_nodes_kernel(positions_ref, pair_nodes_ref, nodes_ref):
    owned_rows = positions_ref.shape[1] // LANES
    for g in range(pair_nodes_ref.shape[0] // 8):
        index = pair_nodes_ref[g * 8 : (g + 1) * 8, :]
        zeros = [jnp.zeros(index.shape, jnp.float32)] * 3
        found = gather_rows(position_row(positions_ref), 0, owned_rows, index, zeros)
        for r in range(3):
            nodes_ref[r, g * 8 : (g + 1) * 8, :] = found[r]


def spread_rows(high_row, parts, rows):
    tiles, place = [], {}
    full, rest = divmod(rows, 16)
    for i, part in enumerate(parts):
        packed = jnp.broadcast_to(part, (16, LANES)).astype(jnp.bfloat16)
        parts[i] = packed
    high = jnp.broadcast_to(high_row, (16, LANES)).astype(jnp.bfloat16)
    zero = jnp.zeros((16, LANES), jnp.bfloat16)
    row = row_iota(16)
    for f in range(full):
        mask = (high - 16.0 * f) == row
        for i, part in enumerate(parts):
            place.update({(i, 16 * f + h): len(tiles) * 16 + h for h in range(16)})
            tiles.append(jnp.where(mask, part, zero))
    if rest:
        share = 16 // rest
        for first in range(0, len(parts), share):
            tile = zero
            for j, i in enumerate(range(first, min(first + share, len(parts)))):
                place.update({(i, 16 * full + h): len(tiles) * 16 + j * rest + h for h in range(rest)})
                shifted = high - (16.0 * full - j * rest)
                mask = (shifted == row) & (high >= 16.0 * full)
                mask = mask & (high < 16.0 * full + rest)
                tile = jnp.where(mask, parts[i], tile)
            tiles.append(tile)
    return jnp.concatenate(tiles, axis=0), place


def column_sums(node_ref, pair_nodes_ref, rows):
    left, right = [], []
    place = None
    for p in range(pair_nodes_ref.shape[0]):
        index = pair_nodes_ref[p : p + 1, :]
        parts = [part[r : r + 1, :] for part in split_two(node_ref[p * 8 : (p + 1) * 8, :]) for r in range(3)]
        spread, place = spread_rows((index >> 7).astype(jnp.float32), parts, rows)
        left.append(spread)
        right.append(one_hot((index & (LANES - 1)).astype(jnp.float32), LANES))
    total = contract_lanes(jnp.concatenate(left, axis=1), jnp.concatenate(right, axis=1))

    def row(r, h):
        upper, lower = place[r, h], place[3 + r, h]
        return total[upper : upper + 1, :] + total[lower : lower + 1, :]

    return row


def gradient_kernel(
    start_ref, ghost_ref, pair_nodes_ref, corner_ref, own_ref, back_ref, place_ref, terms_ref, node_ref, *, dom_count, slot_count
):
    owned_rows = own_ref.shape[1]
    dom_here = lax.axis_index("dom")
    sub_count = ghost_ref.shape[0] // dom_count
    reach = (slot_count - 1) // 2
    pair_count = pair_nodes_ref.shape[0]
    ghost_rows = slot_count * sub_count

    def ghost_place(k):
        return lax.rem(dom_here - k + reach + dom_count, dom_count) * sub_count

    def ghost_row(r, h):
        k, t = divmod(h - owned_rows, sub_count)
        return ghost_ref[pl.ds(ghost_place(k) + t, 1), 0, r * LANES : (r + 1) * LANES]

    def tets_of_pairs(g):
        index = pair_nodes_ref[g * 8 : (g + 1) * 8, :]
        if len(start_ref.shape) == 3:
            nodes = [start_ref[r, g * 8 : (g + 1) * 8, :] for r in range(3)]
        else:
            nodes = [jnp.zeros(index.shape, jnp.float32)] * 3
            nodes = gather_rows(position_row(start_ref), 0, owned_rows, index, nodes)
        nodes = gather_rows(ghost_row, owned_rows, owned_rows + ghost_rows, index, nodes)
        for q in range(2):
            corners = [[None] * 4 for _ in range(3)]
            for n in range(4):
                place = corner_ref[n, pl.ds(g * 16 + q, 8, stride=2), :]
                place_ref[n, pl.ds(g * 16 + q, 8, stride=2), :] = place.astype(jnp.float32)
                for r in range(3):
                    corners[r][n] = lane_gather(nodes[r], place + q * BLOCK_ROWS)
            gradient = distortion_gradient(corners)
            for r in range(3):
                for m in range(3):
                    for s, part in enumerate(split_two(gradient[r][m + 1])):
                        terms_ref[m * 2 + q, pl.ds(g * 64 + s * 4 + r, 8, stride=8), :] = part

    def add_tets(p):
        empty = jnp.zeros((8, LANES), jnp.float32)
        base = [one_hot(place_ref[0, 2 * p + q : 2 * p + q + 1, :], BLOCK_ROWS) for q in range(2)]
        hits, terms = [], []
        for m in range(3):
            for q in range(2):
                hits.append(one_hot(place_ref[m + 1, 2 * p + q : 2 * p + q + 1, :], BLOCK_ROWS) - base[q])
                part = terms_ref[m * 2 + q, p * 8 : (p + 1) * 8, :]
                part = jnp.concatenate([part, empty] if q == 0 else [empty, part], axis=0)
                terms.append(part.astype(jnp.bfloat16))
        sums = contract_lanes(jnp.concatenate(terms, axis=1), jnp.concatenate(hits, axis=1))
        sums = jnp.concatenate([sums[:8], sums[8:]], axis=1)
        node_ref[p * 8 : (p + 1) * 8, :] = sums + pltpu.roll(sums, 4, 0)

    for g in range(pair_count // 8):
        tets_of_pairs(g)
    for p in range(pair_count):
        add_tets(p)
    back_ref[...] = jnp.zeros(back_ref.shape, jnp.float32)
    row = column_sums(node_ref, pair_nodes_ref, owned_rows + ghost_rows)
    for r in range(3):
        for h in range(owned_rows):
            own_ref[r, h : h + 1, :] = row(r, h)
        for k in range(slot_count):
            for t in range(sub_count):
                place = ghost_place(k) + t
                back_ref[pl.ds(place, 1), 0, r * LANES : (r + 1) * LANES] = row(r, owned_rows + k * sub_count + t)


def moved_positions(positions_ref, mask_ref, own_ref, back_ref, list_ref, valid_ref, dom_count):
    dom_here = lax.axis_index("dom")
    slot_count, sub_count, width = list_ref.shape
    reach = (slot_count - 1) // 2
    owned_rows = own_ref.shape[1]
    left, right = [], []
    for k in range(slot_count):
        source = lax.rem(dom_here + k - reach + dom_count, dom_count) * sub_count
        for t in range(sub_count):
            index = list_ref[k, t : t + 1, :]
            valid = valid_ref[k, t : t + 1, :] > 0.0
            mask = row_equals((index >> 7).astype(jnp.float32), owned_rows)
            parts = []
            for r in range(3):
                row = back_ref[pl.ds(source + t, 1), 0, r * LANES : (r + 1) * LANES]
                parts.append(split_two(jnp.where(valid, row, 0.0)))
            left.append(jnp.concatenate([masked_rows(mask, parts[r][s]) for s in range(2) for r in range(3)], axis=0))
            right.append(one_hot((index & (LANES - 1)).astype(jnp.float32), LANES))
    returned = contract_lanes(jnp.concatenate(left, axis=1), jnp.concatenate(right, axis=1))
    free = jnp.where(mask_ref[...] == 0, step_size, 0.0)
    moved = []
    for r in range(3):
        added = returned[r * owned_rows : (r + 1) * owned_rows] + returned[(3 + r) * owned_rows : (4 + r) * owned_rows]
        here = jnp.concatenate(
            [positions_ref[r : r + 1, h * LANES : (h + 1) * LANES] for h in range(owned_rows)], axis=0
        )
        moved.append(here - free * (own_ref[r] + added))
    return moved


def move_kernel(positions_ref, mask_ref, own_ref, back_ref, list_ref, valid_ref, *out_refs, dom_count):
    moved = moved_positions(positions_ref, mask_ref, own_ref, back_ref, list_ref, valid_ref, dom_count)
    owned_rows = own_ref.shape[1]
    for r in range(3):
        for h in range(owned_rows):
            out_refs[0][r : r + 1, h * LANES : (h + 1) * LANES] = moved[r][h : h + 1]
    if len(out_refs) > 1:
        write_payload(lambda r, h: moved[r][h : h + 1], owned_rows, list_ref, valid_ref, out_refs[1], dom_count)


def per_device(positions, fixed_mask, send_count, send_list, block_nodes, tet_corners):
    node_count = positions.shape[1]
    slot_count, sub_count, width = send_list.shape[2:]
    dom_count = lax.axis_size("dom")
    block_count = block_nodes.shape[1]
    owned_rows = node_count // LANES
    counts = send_count[0, 0].T
    lists = send_list[0, 0]
    mask_rows = fixed_mask.reshape(owned_rows, LANES)
    pair_nodes = block_nodes.T.reshape(block_count // 2, LANES)
    corners = tet_corners.reshape(4, block_count, LANES)

    vmem = pl.BlockSpec(memory_space=pltpu.VMEM)
    hbm = pl.BlockSpec(memory_space=pl.ANY)
    exchange_shape = jax.ShapeDtypeStruct((dom_count * sub_count, 1, 3 * LANES), jnp.float32)
    position_shape = jax.ShapeDtypeStruct(positions.shape, jnp.float32)
    params = pltpu.CompilerParams(vmem_limit_bytes=32 * 1024 * 1024)

    def call(kernel, name, ins, outs, scratch=(), **sizes):
        return pl.pallas_call(
            functools.partial(kernel, **sizes),
            out_shape=outs,
            in_specs=ins,
            out_specs=jax.tree.map(lambda _: vmem, outs),
            scratch_shapes=scratch,
            compiler_params=params,
            name=name,
        )

    send = call(
        send_kernel,
        "send",
        [hbm] * 3,
        (exchange_shape, jax.ShapeDtypeStruct(lists.shape, jnp.float32)),
        [
            pltpu.VMEM(positions.shape, jnp.float32),
            pltpu.VMEM(lists.shape, jnp.int32),
            pltpu.VMEM(counts.shape, jnp.int32),
            pltpu.SemaphoreType.DMA((3,)),
        ],
        dom_count=dom_count,
    )
    owned_nodes = call(
        owned_nodes_kernel, "owned_nodes", [vmem] * 2, jax.ShapeDtypeStruct((3,) + pair_nodes.shape, jnp.float32)
    )
    own_shape = jax.ShapeDtypeStruct((3, owned_rows, LANES), jnp.float32)
    gradient = call(
        gradient_kernel,
        "gradient",
        [vmem] * 4,
        (own_shape, exchange_shape),
        [
            pltpu.VMEM((4, block_count, LANES), jnp.float32),
            pltpu.VMEM((6, block_count * 4, LANES), jnp.float32),
            pltpu.VMEM((block_count * 4, LANES), jnp.float32),
        ],
        dom_count=dom_count,
        slot_count=slot_count,
    )

    def exchange(rows):
        return lax.all_to_all(rows, ("dom", "sub"), 0, 0, tiled=True)

    payload, valid = send(*[pltpu.with_memory_space_constraint(x, pltpu.HBM) for x in (positions, lists, counts)])
    for step in range(ITERS):
        last = step == ITERS - 1
        ghosts = exchange(payload)
        start = owned_nodes(positions, pair_nodes) if step == 0 else positions
        own, back = gradient(start, ghosts, pair_nodes, corners)
        returned = exchange(back)
        move = call(
            move_kernel,
            "move_last" if last else "move",
            [vmem] * 6,
            (position_shape,) if last else (position_shape, exchange_shape),
            dom_count=dom_count,
        )
        moved = move(positions, mask_rows, own, returned, lists, valid)
        positions = moved[0]
        if not last:
            payload = moved[1]
    return positions


def solution(mesh):
    return jax.shard_map(
        per_device,
        mesh=mesh,
        in_specs=(
            P(None, ("dom", "sub")),
            P(("dom", "sub")),
            P("dom", "sub", None, None),
            P("dom", "sub", None, None, None),
            P(None, ("dom", "sub")),
            P(None, ("dom", "sub")),
        ),
        out_specs=P(None, ("dom", "sub")),
        check_vma=False,
    )
```

time: 57.4 us -> 52.1 us (0.908)
  Pallas kernels: 12.9 us -> 10.5 us
  local copies, waits for them, and re-layouts: 3.19 us -> 1.64 us
  waiting for transfers between devices: 6.37 us -> 5.18 us
    pallas_call x5 -> x6, Pallas kernels: 12.9 us -> 10.5 us  [the longest x2 6.69 us: per_device(): own, back = gradient(start, ghosts, pair_nodes, corners)]
    all_to_all x1, waiting for transfers between devices: 6.37 us -> 5.18 us  [exchange(): return lax.all_to_all(rows, ('dom', 'sub'), 0, 0, tiled=True)]
    unnamed x13 -> x9, local copies, waits for them, and re-layouts: 1.5 us -> 0.72 us
    squeeze x1 -> x0, local copies, waits for them, and re-layouts: 0.77 us -> none  [per_device(): counts = send_count[0, 0]]
  transfers between devices with their start and end apart: 1 -> 1, of which waited for: 1 -> 1; matrix products, arithmetic and copies ran while one was open for 2% -> 2% of each run, Pallas kernels for 0% -> 1%
where the time goes in v3:
time: 52.1 us; the launch traced here: 51.8 us
  blocking collectives  27.1 us (52%)
  Pallas kernels  10.5 us (20%)
  starting transfers between devices  7.3 us (14%)
  waiting for transfers between devices  5.18 us (10%)
  local copies, waits for them, and re-layouts  1.64 us (3%)
    all_to_all x3, blocking collectives, exchange(): return lax.all_to_all(rows, ('dom', 'sub'), 0, 0, tiled=True)  27.1 us
    all_to_all x1, starting transfers between devices, exchange(): return lax.all_to_all(rows, ('dom', 'sub'), 0, 0, tiled=True)  7.3 us
    pallas_call x2, Pallas kernels, per_device(): own, back = gradient(start, ghosts, pair_nodes, corners)  6.69 us
    all_to_all x1, waiting for transfers between devices, exchange(): return lax.all_to_all(rows, ('dom', 'sub'), 0, 0, tiled=True)  5.18 us
    pallas_call x1, Pallas kernels, per_device(): send(*[pltpu.with_memory_space_constraint(x, pltpu.HBM) for x in (positio...  1.69 us
    pallas_call x2, Pallas kernels, per_device(): moved = move(positions, mask_rows, own, returned, lists, valid)  1.6 us
  transfers between devices with their start and end apart: 1, of which 1 were waited for; matrix products, arithmetic and copies ran while one was open for 2% of the time, Pallas kernels for 1%

profile of v3, /device:TPU:0, one launch (start us, length us, event | category | flops | bytes accessed | tf_op | source)
XLA Modules:
  0.0 51.8 jit_solution(17790363853503377698)
XLA Ops:
  0.0 0.0 copy-start.3
  0.0 1.7 %send.1 = (f32[32,1,384]{2,1,0:T(1,128)}, f32[5,4,128]{2,1,0:T(4,128)S(1)}) custom-call(f32[3,2048]{1,0:T(4,128)} %positions_ref.3, s32[5,4,128]{2,1,0:T(4,128)} %bitcast.12, s32[4,5]{1,0:T(4,128)} %bitcast.19), custom_call_target="tpu_custom_call" | custom-call | tf_op jit(solution)/shard_map/send/pallas_call | solution.py:380
  1.7 7.3 %all-to-all-start = ((f32[32,1,384]{2,1,0:T(1,128)}), f32[32,1,384]{2,1,0:T(1,128)S(1)}, u32[]{:S(2)}, u32[]{:S(2)}) async-start(f32[32,1,384]{2,1,0:T(1,128)} %get-tuple-element.13), calls=%async_computation | async-start | bytes 98304 | tf_op jit(solution)/shard_map/all_to_all | solution.py:378
  9.0 0.8 %copy.8 = s32[128,64]{1,0:T(8,128)S(1)} copy(s32[128,64]{0,1:T(8,128)} %bitcast.18) | data formatting | bytes 65536 | tf_op jit(solution)/shard_map/transpose | solution.py:326
  9.9 0.0 copy-start
  9.9 0.1 reshape.10.pair_nodes_ref
  10.0 0.7 %copy-done = f32[3,2048]{1,0:T(4,128)S(1)} copy-done((f32[3,2048]{1,0:T(4,128)S(1)}, f32[3,2048]{1,0:T(4,128)}, u32[]{:S(2)}) %copy-start) | copy-done | bytes 24600
  10.6 0.5 owned_nodes.1.start_ref
  11.1 0.0 copy-done.3
  11.2 5.2 %all-to-all-done.ghost_ref = f32[32,1,384]{2,1,0:T(1,128)S(1)} async-done(((f32[32,1,384]{2,1,0:T(1,128)}), f32[32,1,384]{2,1,0:T(1,128)S(1)}, u32[]{:S(2)}, u32[]{:S(2)}) %all-to-all-start) | async-done | bytes 49184 | tf_op jit(solution)/shard_map/all_to_all | solution.py:378
  16.3 3.2 %gradient.2 = (f32[3,16,128]{2,1,0:T(8,128)S(1)}, f32[32,1,384]{2,1,0:T(1,128)S(1)}) custom-call(f32[3,64,128]{2,1,0:T(8,128)S(1)} %owned_nodes.1.start_ref, f32[32,1,384]{2,1,0:T(1,128)S(1)} %all-to-all-done.ghost_ref, s32[64,128]{1,0:T(8,128)S(1)} %reshape.10.pair_nodes_ref, s32[4,128,128]{2,1,0:T(8,128)S(1)} %bitcast.10), custom_call_target="tpu_custom_call" | custom-call | tf_op jit(solution)/shard_map/gradient/pallas_call | solution.py:385
  19.5 0.0 copy-start.1
  19.5 0.0 copy-start.2
  19.5 9.0 %all_to_all.20.back_ref = f32[32,1,384]{2,1,0:T(1,128)S(1)} all-to-all(f32[32,1,384]{2,1,0:T(1,128)S(1)} %get-tuple-element.15), channel_id=1, replica_groups=mesh['dom'=8,'sub'=4] {'dom','sub'}, dimensions={0} | all-to-all | bytes 98304 | tf_op jit(solution)/shard_map/all_to_all | solution.py:378
  28.6 0.0 copy-done.1
  28.6 0.0 copy-done.2
  28.6 0.6 %move.1 = (f32[3,2048]{1,0:T(4,128)S(1)}, f32[32,1,384]{2,1,0:T(1,128)S(1)}) custom-call(f32[3,2048]{1,0:T(4,128)S(1)} %copy-done, s32[16,128]{1,0:T(8,128)S(1)} %bitcast.15, f32[3,16,128]{2,1,0:T(8,128)S(1)} %get-tuple-element.14.own_ref, f32[32,1,384]{2,1,0:T(1,128)S(1)} %all_to_all.20.back_ref, s32[5,4,128]{2,1,0:T(4,128)S(1)} %bitcast.13, ...), custom_call_target="tpu_custom_call" | custom-call | tf_op jit(solution)/shard_map/move/pallas_call | solution.py:394
  29.2 9.0 %all_to_all.21.ghost_ref = f32[32,1,384]{2,1,0:T(1,128)S(1)} all-to-all(f32[32,1,384]{2,1,0:T(1,128)S(1)} %get-tuple-element.18), channel_id=1, replica_groups=mesh['dom'=8,'sub'=4] {'dom','sub'}, dimensions={0} | all-to-all | bytes 98304 | tf_op jit(solution)/shard_map/all_to_all | solution.py:378
  38.2 3.5 %gradient.3 = (f32[3,16,128]{2,1,0:T(8,128)S(1)}, f32[32,1,384]{2,1,0:T(1,128)S(1)}) custom-call(f32[3,2048]{1,0:T(4,128)S(1)} %get-tuple-element.17.start_ref.positions_ref, f32[32,1,384]{2,1,0:T(1,128)S(1)} %all_to_all.21.ghost_ref, s32[64,128]{1,0:T(8,128)S(1)} %reshape.10.pair_nodes_ref, s32[4,128,128]{2,1,0:T(8,128)S(1)} %bitcast.11), custom_call_target="tpu_custom_call" | custom-call | tf_op jit(solution)/shard_map/gradient/pallas_call | solution.py:385
  41.7 9.0 %all_to_all.22.back_ref = f32[32,1,384]{2,1,0:T(1,128)S(1)} all-to-all(f32[32,1,384]{2,1,0:T(1,128)S(1)} %get-tuple-element.20), channel_id=1, replica_groups=mesh['dom'=8,'sub'=4] {'dom','sub'}, dimensions={0} | all-to-all | bytes 98304 | tf_op jit(solution)/shard_map/all_to_all | solution.py:378
  50.8 1.0 %move_last.1 = f32[3,2048]{1,0:T(4,128)} custom-call(f32[3,2048]{1,0:T(4,128)S(1)} %get-tuple-element.17.start_ref.positions_ref, s32[16,128]{1,0:T(8,128)S(1)} %bitcast.16, f32[3,16,128]{2,1,0:T(8,128)S(1)} %get-tuple-element.19.own_ref, f32[32,1,384]{2,1,0:T(1,128)S(1)} %all_to_all.22.back_ref, s32[5,4,128]{2,1,0:T(4,128)S(1)} %bitcast.14, ...), custom_call_target="tpu_custom_call" | custom-call | tf_op jit(solution)/shard_map/move_last/pallas_call | solution.py:394
  (1 shorter events, 0.0 us)
Async XLA Ops:
  0.0 11.1 %copy-start.3 = (s32[4,16384]{1,0:T(4,128)S(1)}, s32[4,16384]{1,0:T(4,128)}, u32[]{:S(2)}) copy-start(s32[4,16384]{1,0:T(4,128)} %param.11) | copy-start | bytes 786436
  1.7 14.6 %all-to-all-start = ((f32[32,1,384]{2,1,0:T(1,128)}), f32[32,1,384]{2,1,0:T(1,128)S(1)}, u32[]{:S(2)}, u32[]{:S(2)}) async-start(f32[32,1,384]{2,1,0:T(1,128)} %get-tuple-element.13), calls=%async_computation | async-start | bytes 98304 | tf_op jit(solution)/shard_map/all_to_all | solution.py:378
  9.9 0.8 %copy-start = (f32[3,2048]{1,0:T(4,128)S(1)}, f32[3,2048]{1,0:T(4,128)}, u32[]{:S(2)}) copy-start(f32[3,2048]{1,0:T(4,128)} %positions_ref.3) | copy-start | bytes 73732
  19.5 9.1 %copy-start.1 = (s32[1,1,5,4,128]{4,3,2,1,0:T(4,128)S(1)}, s32[1,1,5,4,128]{4,3,2,1,0:T(4,128)}, u32[]{:S(2)}) copy-start(s32[1,1,5,4,128]{4,3,2,1,0:T(4,128)} %param.9) | copy-start | bytes 30724
  19.5 9.0 %copy-start.2 = (s32[2048]{0:T(1024)S(1)}, s32[2048]{0:T(1024)}, u32[]{:S(2)}) copy-start(s32[2048]{0:T(1024)} %param.7) | copy-start | bytes 24580

commit v4 on v3

--- a/solution.py
+++ b/solution.py
@@ -39,13 +39,13 @@
 
 
 def row_equals(ids_row, rows):
-    packed = jnp.broadcast_to(ids_row, (16, LANES)).astype(jnp.bfloat16)
-    return jnp.concatenate([packed] * (rows // 16), axis=0) == row_iota(rows)
-
-
-def one_hot(ids_row, rows):
+    packed = jnp.broadcast_to(ids_row, (16, LANES)).astype(jnp.int16)
+    return jnp.concatenate([packed] * (rows // 16), axis=0) == lax.broadcasted_iota(jnp.int32, (rows, LANES), 0).astype(jnp.int16)
+
+
+def one_hot(ids_row, rows, value=1.0):
     mask = row_equals(ids_row, rows)
-    return jnp.where(mask, jnp.ones((rows, LANES), jnp.bfloat16), jnp.zeros((rows, LANES), jnp.bfloat16))
+    return jnp.where(mask, jnp.full((rows, LANES), value, jnp.bfloat16), jnp.zeros((rows, LANES), jnp.bfloat16))
 
 
 def split_two(values):
@@ -130,16 +130,39 @@
                     out_ref[pl.ds(target + t, 1), 0, r * LANES : (r + 1) * LANES] = row
 
 
-def send_kernel(positions_hbm, list_hbm, count_hbm, out_ref, valid_ref, positions_ref, list_ref, count_ref, sems, *, dom_count):
+def send_kernel(
+    positions_hbm,
+    list_hbm,
+    count_hbm,
+    block_nodes_hbm,
+    corner_hbm,
+    out_ref,
+    valid_ref,
+    pair_nodes_ref,
+    corner_ref,
+    positions_ref,
+    list_ref,
+    count_ref,
+    block_nodes_ref,
+    sems,
+    *,
+    dom_count,
+):
     copies = [
         pltpu.make_async_copy(source, target, sems.at[i])
         for i, (source, target) in enumerate(
-            [(positions_hbm, positions_ref), (list_hbm, list_ref), (count_hbm, count_ref)]
+            [
+                (positions_hbm, positions_ref),
+                (list_hbm, list_ref),
+                (count_hbm, count_ref),
+                (block_nodes_hbm, block_nodes_ref),
+                (corner_hbm, corner_ref),
+            ]
         )
     ]
     for copy in copies:
         copy.start()
-    for copy in copies:
+    for copy in copies[:3]:
         copy.wait()
     slot_count, sub_count, width = list_ref.shape
     lane = lax.broadcasted_iota(jnp.int32, (sub_count, LANES), 1)
@@ -149,42 +172,36 @@
     write_payload(
         position_row(positions_ref), positions_ref.shape[1] // LANES, list_ref, valid_ref, out_ref, dom_count
     )
-
-
-def owned_nodes_kernel(positions_ref, pair_nodes_ref, nodes_ref):
-    owned_rows = positions_ref.shape[1] // LANES
-    for g in range(pair_nodes_ref.shape[0] // 8):
-        index = pair_nodes_ref[g * 8 : (g + 1) * 8, :]
-        zeros = [jnp.zeros(index.shape, jnp.float32)] * 3
-        found = gather_rows(position_row(positions_ref), 0, owned_rows, index, zeros)
-        for r in range(3):
-            nodes_ref[r, g * 8 : (g + 1) * 8, :] = found[r]
+    copies[3].wait()
+    half = pair_nodes_ref.shape[0]
+    nodes = block_nodes_ref[...].T
+    pair_nodes_ref[...] = jnp.concatenate([nodes[:half], nodes[half:]], axis=1)
+    copies[4].wait()
 
 
 def spread_rows(high_row, parts, rows):
     tiles, place = [], {}
     full, rest = divmod(rows, 16)
-    for i, part in enumerate(parts):
-        packed = jnp.broadcast_to(part, (16, LANES)).astype(jnp.bfloat16)
-        parts[i] = packed
+    parts = [jnp.broadcast_to(part, (16, LANES)).astype(jnp.bfloat16) for part in parts]
     high = jnp.broadcast_to(high_row, (16, LANES)).astype(jnp.bfloat16)
     zero = jnp.zeros((16, LANES), jnp.bfloat16)
-    row = row_iota(16)
+    row = lax.broadcasted_iota(jnp.int32, (16, LANES), 0)
     for f in range(full):
-        mask = (high - 16.0 * f) == row
+        mask = high == (row + 16 * f).astype(jnp.float32).astype(jnp.bfloat16)
         for i, part in enumerate(parts):
             place.update({(i, 16 * f + h): len(tiles) * 16 + h for h in range(16)})
             tiles.append(jnp.where(mask, part, zero))
     if rest:
         share = 16 // rest
+        masks = []
+        for j in range(share):
+            wanted = jnp.where((row >= j * rest) & (row < (j + 1) * rest), row - j * rest + 16 * full, -1)
+            masks.append(high == wanted.astype(jnp.float32).astype(jnp.bfloat16))
         for first in range(0, len(parts), share):
             tile = zero
             for j, i in enumerate(range(first, min(first + share, len(parts)))):
                 place.update({(i, 16 * full + h): len(tiles) * 16 + j * rest + h for h in range(rest)})
-                shifted = high - (16.0 * full - j * rest)
-                mask = (shifted == row) & (high >= 16.0 * full)
-                mask = mask & (high < 16.0 * full + rest)
-                tile = jnp.where(mask, parts[i], tile)
+                tile = jnp.where(masks[j], parts[i], tile)
             tiles.append(tile)
     return jnp.concatenate(tiles, axis=0), place
 
@@ -197,7 +214,7 @@
         parts = [part[r : r + 1, :] for part in split_two(node_ref[p * 8 : (p + 1) * 8, :]) for r in range(3)]
         spread, place = spread_rows((index >> 7).astype(jnp.float32), parts, rows)
         left.append(spread)
-        right.append(one_hot((index & (LANES - 1)).astype(jnp.float32), LANES))
+        right.append(one_hot(index & (LANES - 1), LANES))
     total = contract_lanes(jnp.concatenate(left, axis=1), jnp.concatenate(right, axis=1))
 
     def row(r, h):
@@ -208,7 +225,7 @@
 
 
 def gradient_kernel(
-    start_ref, ghost_ref, pair_nodes_ref, corner_ref, own_ref, back_ref, place_ref, terms_ref, node_ref, *, dom_count, slot_count
+    positions_ref, ghost_ref, pair_nodes_ref, corner_ref, own_ref, back_ref, terms_ref, node_ref, *, dom_count, slot_count
 ):
     owned_rows = own_ref.shape[1]
     dom_here = lax.axis_index("dom")
@@ -226,17 +243,14 @@
 
     def tets_of_pairs(g):
         index = pair_nodes_ref[g * 8 : (g + 1) * 8, :]
-        if len(start_ref.shape) == 3:
-            nodes = [start_ref[r, g * 8 : (g + 1) * 8, :] for r in range(3)]
-        else:
-            nodes = [jnp.zeros(index.shape, jnp.float32)] * 3
-            nodes = gather_rows(position_row(start_ref), 0, owned_rows, index, nodes)
+        nodes = [jnp.zeros(index.shape, jnp.float32)] * 3
+        nodes = gather_rows(position_row(positions_ref), 0, owned_rows, index, nodes)
         nodes = gather_rows(ghost_row, owned_rows, owned_rows + ghost_rows, index, nodes)
         for q in range(2):
             corners = [[None] * 4 for _ in range(3)]
             for n in range(4):
-                place = corner_ref[n, pl.ds(g * 16 + q, 8, stride=2), :]
-                place_ref[n, pl.ds(g * 16 + q, 8, stride=2), :] = place.astype(jnp.float32)
+                first = q * pair_count + g * 8
+                place = corner_ref[first : first + 8, n, :]
                 for r in range(3):
                     corners[r][n] = lane_gather(nodes[r], place + q * BLOCK_ROWS)
             gradient = distortion_gradient(corners)
@@ -247,11 +261,13 @@
 
     def add_tets(p):
         empty = jnp.zeros((8, LANES), jnp.float32)
-        base = [one_hot(place_ref[0, 2 * p + q : 2 * p + q + 1, :], BLOCK_ROWS) for q in range(2)]
+        blocks = [p, pair_count + p]
+        base = [one_hot(corner_ref[b, 0:1, :], BLOCK_ROWS, -1.0) for b in blocks]
         hits, terms = [], []
         for m in range(3):
             for q in range(2):
-                hits.append(one_hot(place_ref[m + 1, 2 * p + q : 2 * p + q + 1, :], BLOCK_ROWS) - base[q])
+                hit = row_equals(corner_ref[blocks[q], m + 1 : m + 2, :], BLOCK_ROWS)
+                hits.append(jnp.where(hit, jnp.ones_like(base[q]), base[q]))
                 part = terms_ref[m * 2 + q, p * 8 : (p + 1) * 8, :]
                 part = jnp.concatenate([part, empty] if q == 0 else [empty, part], axis=0)
                 terms.append(part.astype(jnp.bfloat16))
@@ -285,13 +301,13 @@
         for t in range(sub_count):
             index = list_ref[k, t : t + 1, :]
             valid = valid_ref[k, t : t + 1, :] > 0.0
-            mask = row_equals((index >> 7).astype(jnp.float32), owned_rows)
+            mask = row_equals(index >> 7, owned_rows)
             parts = []
             for r in range(3):
                 row = back_ref[pl.ds(source + t, 1), 0, r * LANES : (r + 1) * LANES]
                 parts.append(split_two(jnp.where(valid, row, 0.0)))
             left.append(jnp.concatenate([masked_rows(mask, parts[r][s]) for s in range(2) for r in range(3)], axis=0))
-            right.append(one_hot((index & (LANES - 1)).astype(jnp.float32), LANES))
+            right.append(one_hot(index & (LANES - 1), LANES))
     returned = contract_lanes(jnp.concatenate(left, axis=1), jnp.concatenate(right, axis=1))
     free = jnp.where(mask_ref[...] == 0, step_size, 0.0)
     moved = []
@@ -323,8 +339,7 @@
     counts = send_count[0, 0].T
     lists = send_list[0, 0]
     mask_rows = fixed_mask.reshape(owned_rows, LANES)
-    pair_nodes = block_nodes.T.reshape(block_count // 2, LANES)
-    corners = tet_corners.reshape(4, block_count, LANES)
+    corners = tet_corners.reshape(4, block_count, LANES).transpose(1, 0, 2)
 
     vmem = pl.BlockSpec(memory_space=pltpu.VMEM)
     hbm = pl.BlockSpec(memory_space=pl.ANY)
@@ -346,18 +361,21 @@
     send = call(
         send_kernel,
         "send",
-        [hbm] * 3,
-        (exchange_shape, jax.ShapeDtypeStruct(lists.shape, jnp.float32)),
+        [hbm] * 5,
+        (
+            exchange_shape,
+            jax.ShapeDtypeStruct(lists.shape, jnp.float32),
+            jax.ShapeDtypeStruct((block_count // 2, LANES), jnp.int32),
+            jax.ShapeDtypeStruct(corners.shape, jnp.int32),
+        ),
         [
             pltpu.VMEM(positions.shape, jnp.float32),
             pltpu.VMEM(lists.shape, jnp.int32),
             pltpu.VMEM(counts.shape, jnp.int32),
-            pltpu.SemaphoreType.DMA((3,)),
+            pltpu.VMEM(block_nodes.shape, jnp.int32),
+            pltpu.SemaphoreType.DMA((5,)),
         ],
         dom_count=dom_count,
-    )
-    owned_nodes = call(
-        owned_nodes_kernel, "owned_nodes", [vmem] * 2, jax.ShapeDtypeStruct((3,) + pair_nodes.shape, jnp.float32)
     )
     own_shape = jax.ShapeDtypeStruct((3, owned_rows, LANES), jnp.float32)
     gradient = call(
@@ -366,7 +384,6 @@
         [vmem] * 4,
         (own_shape, exchange_shape),
         [
-            pltpu.VMEM((4, block_count, LANES), jnp.float32),
             pltpu.VMEM((6, block_count * 4, LANES), jnp.float32),
             pltpu.VMEM((block_count * 4, LANES), jnp.float32),
         ],
@@ -377,12 +394,12 @@
     def exchange(rows):
         return lax.all_to_all(rows, ("dom", "sub"), 0, 0, tiled=True)
 
-    payload, valid = send(*[pltpu.with_memory_space_constraint(x, pltpu.HBM) for x in (positions, lists, counts)])
+    inputs = (positions, lists, counts, block_nodes, corners)
+    payload, valid, pair_nodes, corners = send(*[pltpu.with_memory_space_constraint(x, pltpu.HBM) for x in inputs])
     for step in range(ITERS):
         last = step == ITERS - 1
         ghosts = exchange(payload)
-        start = owned_nodes(positions, pair_nodes) if step == 0 else positions
-        own, back = gradient(start, ghosts, pair_nodes, corners)
+        own, back = gradient(positions, ghosts, pair_nodes, corners)
         returned = exchange(back)
         move = call(
             move_kernel,

time: 52.1 us -> 51.8 us (level)
  blocking collectives: 27.1 us -> 41.5 us
  starting transfers between devices: 7.3 us -> 0 us
  waiting for transfers between devices: 5.18 us -> 0 us
  local copies, waits for them, and re-layouts: 1.64 us -> 0.02 us
  Pallas kernels: 10.5 us -> 9.9 us
    all_to_all x3 -> x4, blocking collectives: 27.1 us -> 41.5 us  [exchange(): return lax.all_to_all(rows, ('dom', 'sub'), 0, 0, tiled=True)]
    all_to_all x1 -> x0, starting transfers between devices: 7.3 us -> none  [exchange(): return lax.all_to_all(rows, ('dom', 'sub'), 0, 0, tiled=True)]
    all_to_all x1 -> x0, waiting for transfers between devices: 5.18 us -> none  [exchange(): return lax.all_to_all(rows, ('dom', 'sub'), 0, 0, tiled=True)]
    transpose x1 -> x0, local copies, waits for them, and re-layouts: 0.85 us -> none  [per_device(): pair_nodes = block_nodes.T.reshape(block_count // 2, LANES)]
    unnamed x9 -> x6, local copies, waits for them, and re-layouts: 0.72 us -> 0.02 us
    pallas_call x4 -> x3, Pallas kernels: 8.86 us -> 8.31 us  [the longest x2 7.1 us: per_device(): own, back = gradient(positions, ghosts, pair_nodes, corners)]
  transfers between devices with their start and end apart: 1 -> 0, of which waited for: 1 -> 0; matrix products, arithmetic and copies ran while one was open for 2% -> 0% of each run, Pallas kernels for 1% -> 0%
where the time goes in v4:
time: 51.8 us; the launch traced here: 51.5 us
  blocking collectives  41.5 us (80%)
  Pallas kernels  9.9 us (19%)
    all_to_all x4, blocking collectives, exchange(): return lax.all_to_all(rows, ('dom', 'sub'), 0, 0, tiled=True)  41.5 us
    pallas_call x2, Pallas kernels, per_device(): own, back = gradient(positions, ghosts, pair_nodes, corners)  7.1 us
    pallas_call x2, Pallas kernels, per_device(): moved = move(positions, mask_rows, own, returned, lists, valid)  1.59 us
    pallas_call x1, Pallas kernels, per_device(): send(*[pltpu.with_memory_space_constraint(x, pltpu.HBM) for x in inputs])  1.21 us

profile of v4, /device:TPU:0, one launch (start us, length us, event | category | flops | bytes accessed | tf_op | source)
XLA Modules:
  0.0 51.5 jit_solution(12546641011999250196)
XLA Ops:
  0.0 1.2 %send.1 = (f32[32,1,384]{2,1,0:T(1,128)S(1)}, f32[5,4,128]{2,1,0:T(4,128)S(1)}, s32[64,128]{1,0:T(8,128)S(1)}, s32[128,4,128]{2,1,0:T(4,128)S(1)}) custom-call(f32[3,2048]{1,0:T(4,128)} %positions_ref.3, s32[5,4,128]{2,1,0:T(4,128)} %bitcast.8, s32[4,5]{1,0:T(4,128)} %bitcast.14, s32[64,128]{1,0:T(8,128)} %block_nodes_hbm.1, s32[128,4,128]{2,1,0:T(4,128)} %bitcast.13), custom_call_target="tpu_custom_call" | custom-call | tf_op jit(solution)/shard_map/send/pallas_call | solution.py:398
  1.2 0.0 copy-start
  1.2 14.4 %all_to_all.20.ghost_ref = f32[32,1,384]{2,1,0:T(1,128)S(1)} all-to-all(f32[32,1,384]{2,1,0:T(1,128)S(1)} %get-tuple-element.15), channel_id=1, replica_groups=mesh['dom'=8,'sub'=4] {'dom','sub'}, dimensions={0} | all-to-all | bytes 98304 | tf_op jit(solution)/shard_map/all_to_all | solution.py:395
  15.7 0.0 copy-done
  15.7 3.5 %gradient.2 = (f32[3,16,128]{2,1,0:T(8,128)S(1)}, f32[32,1,384]{2,1,0:T(1,128)S(1)}) custom-call(f32[3,2048]{1,0:T(4,128)S(1)} %copy-done, f32[32,1,384]{2,1,0:T(1,128)S(1)} %all_to_all.20.ghost_ref, s32[64,128]{1,0:T(8,128)S(1)} %get-tuple-element.16.pair_nodes_ref, s32[128,4,128]{2,1,0:T(4,128)S(1)} %get-tuple-element.17.corner_ref), custom_call_target="tpu_custom_call" | custom-call | tf_op jit(solution)/shard_map/gradient/pallas_call | solution.py:402
  19.2 0.0 copy-start.1
  19.2 0.0 copy-start.2
  19.2 9.0 %all_to_all.21.back_ref = f32[32,1,384]{2,1,0:T(1,128)S(1)} all-to-all(f32[32,1,384]{2,1,0:T(1,128)S(1)} %get-tuple-element.19), channel_id=1, replica_groups=mesh['dom'=8,'sub'=4] {'dom','sub'}, dimensions={0} | all-to-all | bytes 98304 | tf_op jit(solution)/shard_map/all_to_all | solution.py:395
  28.3 0.0 copy-done.1
  28.3 0.0 copy-done.2
  28.3 0.6 %move.1 = (f32[3,2048]{1,0:T(4,128)S(1)}, f32[32,1,384]{2,1,0:T(1,128)S(1)}) custom-call(f32[3,2048]{1,0:T(4,128)S(1)} %copy-done, s32[16,128]{1,0:T(8,128)S(1)} %bitcast.11, f32[3,16,128]{2,1,0:T(8,128)S(1)} %get-tuple-element.18.own_ref, f32[32,1,384]{2,1,0:T(1,128)S(1)} %all_to_all.21.back_ref, s32[5,4,128]{2,1,0:T(4,128)S(1)} %bitcast.9, ...), custom_call_target="tpu_custom_call" | custom-call | tf_op jit(solution)/shard_map/move/pallas_call | solution.py:411
  28.9 9.0 %all_to_all.22.ghost_ref = f32[32,1,384]{2,1,0:T(1,128)S(1)} all-to-all(f32[32,1,384]{2,1,0:T(1,128)S(1)} %get-tuple-element.22), channel_id=1, replica_groups=mesh['dom'=8,'sub'=4] {'dom','sub'}, dimensions={0} | all-to-all | bytes 98304 | tf_op jit(solution)/shard_map/all_to_all | solution.py:395
  37.9 3.6 %gradient.3 = (f32[3,16,128]{2,1,0:T(8,128)S(1)}, f32[32,1,384]{2,1,0:T(1,128)S(1)}) custom-call(f32[3,2048]{1,0:T(4,128)S(1)} %get-tuple-element.21.positions_ref, f32[32,1,384]{2,1,0:T(1,128)S(1)} %all_to_all.22.ghost_ref, s32[64,128]{1,0:T(8,128)S(1)} %get-tuple-element.16.pair_nodes_ref, s32[128,4,128]{2,1,0:T(4,128)S(1)} %get-tuple-element.17.corner_ref), custom_call_target="tpu_custom_call" | custom-call | tf_op jit(solution)/shard_map/gradient/pallas_call | solution.py:402
  41.5 9.0 %all_to_all.23.back_ref = f32[32,1,384]{2,1,0:T(1,128)S(1)} all-to-all(f32[32,1,384]{2,1,0:T(1,128)S(1)} %get-tuple-element.24), channel_id=1, replica_groups=mesh['dom'=8,'sub'=4] {'dom','sub'}, dimensions={0} | all-to-all | bytes 98304 | tf_op jit(solution)/shard_map/all_to_all | solution.py:395
  50.5 1.0 %move_last.1 = f32[3,2048]{1,0:T(4,128)} custom-call(f32[3,2048]{1,0:T(4,128)S(1)} %get-tuple-element.21.positions_ref, s32[16,128]{1,0:T(8,128)S(1)} %bitcast.12, f32[3,16,128]{2,1,0:T(8,128)S(1)} %get-tuple-element.23.own_ref, f32[32,1,384]{2,1,0:T(1,128)S(1)} %all_to_all.23.back_ref, s32[5,4,128]{2,1,0:T(4,128)S(1)} %bitcast.10, ...), custom_call_target="tpu_custom_call" | custom-call | tf_op jit(solution)/shard_map/move_last/pallas_call | solution.py:411
Async XLA Ops:
  1.2 14.5 %copy-start = (f32[3,2048]{1,0:T(4,128)S(1)}, f32[3,2048]{1,0:T(4,128)}, u32[]{:S(2)}) copy-start(f32[3,2048]{1,0:T(4,128)} %positions_ref.3) | copy-start | bytes 73732
  19.2 9.1 %copy-start.1 = (s32[1,1,5,4,128]{4,3,2,1,0:T(4,128)S(1)}, s32[1,1,5,4,128]{4,3,2,1,0:T(4,128)}, u32[]{:S(2)}) copy-start(s32[1,1,5,4,128]{4,3,2,1,0:T(4,128)} %param.9) | copy-start | bytes 30724
  19.2 9.0 %copy-start.2 = (s32[2048]{0:T(1024)S(1)}, s32[2048]{0:T(1024)}, u32[]{:S(2)}) copy-start(s32[2048]{0:T(1024)} %param.7) | copy-start | bytes 24580

commit v5 on v4

--- a/solution.py
+++ b/solution.py
@@ -139,11 +139,11 @@
     out_ref,
     valid_ref,
     pair_nodes_ref,
+    block_nodes_ref,
     corner_ref,
     positions_ref,
     list_ref,
     count_ref,
-    block_nodes_ref,
     sems,
     *,
     dom_count,
@@ -206,26 +206,40 @@
     return jnp.concatenate(tiles, axis=0), place
 
 
-def column_sums(node_ref, pair_nodes_ref, rows):
+def column_sums(node_ref, pair_nodes_ref, block_nodes_ref, rows):
+    pair_count = pair_nodes_ref.shape[0]
     left, right = [], []
     place = None
-    for p in range(pair_nodes_ref.shape[0]):
-        index = pair_nodes_ref[p : p + 1, :]
+    low = (block_nodes_ref[...] & (2 * LANES - 1)).astype(jnp.int16)
+    lane = lax.broadcasted_iota(jnp.int32, (BLOCK_ROWS, LANES), 1)
+    lanes = [(lane + i * LANES).astype(jnp.int16) for i in range(2)]
+    ones = jnp.ones((BLOCK_ROWS, LANES), jnp.bfloat16)
+    for p in range(pair_count):
         parts = [part[r : r + 1, :] for part in split_two(node_ref[p * 8 : (p + 1) * 8, :]) for r in range(3)]
-        spread, place = spread_rows((index >> 7).astype(jnp.float32), parts, rows)
+        high = pair_nodes_ref[p : p + 1, :] >> 8
+        spread, place = spread_rows(high.astype(jnp.float32), parts, -(-rows // 2))
         left.append(spread)
-        right.append(one_hot(index & (LANES - 1), LANES))
-    total = contract_lanes(jnp.concatenate(left, axis=1), jnp.concatenate(right, axis=1))
+        for b in (p, pair_count + p):
+            column = jnp.broadcast_to(low[:, b : b + 1], (BLOCK_ROWS, LANES))
+            halves = [jnp.where(column == half, ones, jnp.zeros_like(ones)) for half in lanes]
+            right.append(jnp.concatenate(halves, axis=1))
+    total = lax.dot_general(
+        jnp.concatenate(left, axis=1),
+        jnp.concatenate(right, axis=0),
+        (((1,), (0,)), ((), ())),
+        preferred_element_type=jnp.float32,
+    )
 
     def row(r, h):
-        upper, lower = place[r, h], place[3 + r, h]
-        return total[upper : upper + 1, :] + total[lower : lower + 1, :]
+        upper, lower = place[r, h // 2], place[3 + r, h // 2]
+        half = slice((h % 2) * LANES, (h % 2 + 1) * LANES)
+        return total[upper : upper + 1, half] + total[lower : lower + 1, half]
 
     return row
 
 
 def gradient_kernel(
-    positions_ref, ghost_ref, pair_nodes_ref, corner_ref, own_ref, back_ref, terms_ref, node_ref, *, dom_count, slot_count
+    positions_ref, ghost_ref, pair_nodes_ref, block_nodes_ref, corner_ref, own_ref, back_ref, terms_ref, node_ref, *, dom_count, slot_count
 ):
     owned_rows = own_ref.shape[1]
     dom_here = lax.axis_index("dom")
@@ -280,7 +294,7 @@
     for p in range(pair_count):
         add_tets(p)
     back_ref[...] = jnp.zeros(back_ref.shape, jnp.float32)
-    row = column_sums(node_ref, pair_nodes_ref, owned_rows + ghost_rows)
+    row = column_sums(node_ref, pair_nodes_ref, block_nodes_ref, owned_rows + ghost_rows)
     for r in range(3):
         for h in range(owned_rows):
             own_ref[r, h : h + 1, :] = row(r, h)
@@ -366,13 +380,13 @@
             exchange_shape,
             jax.ShapeDtypeStruct(lists.shape, jnp.float32),
             jax.ShapeDtypeStruct((block_count // 2, LANES), jnp.int32),
+            jax.ShapeDtypeStruct(block_nodes.shape, jnp.int32),
             jax.ShapeDtypeStruct(corners.shape, jnp.int32),
         ),
         [
             pltpu.VMEM(positions.shape, jnp.float32),
             pltpu.VMEM(lists.shape, jnp.int32),
             pltpu.VMEM(counts.shape, jnp.int32),
-            pltpu.VMEM(block_nodes.shape, jnp.int32),
             pltpu.SemaphoreType.DMA((5,)),
         ],
         dom_count=dom_count,
@@ -381,7 +395,7 @@
     gradient = call(
         gradient_kernel,
         "gradient",
-        [vmem] * 4,
+        [vmem] * 5,
         (own_shape, exchange_shape),
         [
             pltpu.VMEM((6, block_count * 4, LANES), jnp.float32),
@@ -395,11 +409,11 @@
         return lax.all_to_all(rows, ("dom", "sub"), 0, 0, tiled=True)
 
     inputs = (positions, lists, counts, block_nodes, corners)
-    payload, valid, pair_nodes, corners = send(*[pltpu.with_memory_space_constraint(x, pltpu.HBM) for x in inputs])
+    payload, valid, pair_nodes, block_nodes, corners = send(*[pltpu.with_memory_space_constraint(x, pltpu.HBM) for x in inputs])
     for step in range(ITERS):
         last = step == ITERS - 1
         ghosts = exchange(payload)
-        own, back = gradient(positions, ghosts, pair_nodes, corners)
+        own, back = gradient(positions, ghosts, pair_nodes, block_nodes, corners)
         returned = exchange(back)
         move = call(
             move_kernel,

time: 51.8 us -> 51 us (0.985)
  Pallas kernels: 9.9 us -> 9.13 us
    pallas_call x2, Pallas kernels: 7.1 us -> 6.32 us  [per_device(): own, back = gradient(positions, ghosts, pair_nodes, block_nodes, corners)]
where the time goes in v5:
time: 51 us; the launch traced here: 50.7 us
  blocking collectives  41.5 us (81%)
  Pallas kernels  9.13 us (18%)
    all_to_all x4, blocking collectives, exchange(): return lax.all_to_all(rows, ('dom', 'sub'), 0, 0, tiled=True)  41.5 us
    pallas_call x2, Pallas kernels, per_device(): own, back = gradient(positions, ghosts, pair_nodes, block_nodes, corners)  6.32 us
    pallas_call x2, Pallas kernels, per_device(): moved = move(positions, mask_rows, own, returned, lists, valid)  1.59 us
    pallas_call x1, Pallas kernels, per_device(): send(*[pltpu.with_memory_space_constraint(x, pltpu.HBM) for x in inputs])  1.21 us

profile of v5, /device:TPU:0, one launch (start us, length us, event | category | flops | bytes accessed | tf_op | source)
XLA Modules:
  0.0 50.7 jit_solution(14197849780356153234)
XLA Ops:
  0.0 1.2 %send.1 = (f32[32,1,384]{2,1,0:T(1,128)S(1)}, f32[5,4,128]{2,1,0:T(4,128)S(1)}, s32[64,128]{1,0:T(8,128)S(1)}, s32[64,128]{1,0:T(8,128)S(1)}, s32[128,4,128]{2,1,0:T(4,128)S(1)}) custom-call(f32[3,2048]{1,0:T(4,128)} %positions_ref.3, s32[5,4,128]{2,1,0:T(4,128)} %bitcast.8, s32[4,5]{1,0:T(4,128)} %bitcast.14, s32[64,128]{1,0:T(8,128)} %block_nodes_hbm.1, ...), custom_call_target="tpu_custom_call" | custom-call | tf_op jit(solution)/shard_map/send/pallas_call | solution.py:412
  1.2 0.0 copy-start
  1.2 14.4 %all_to_all.20.ghost_ref = f32[32,1,384]{2,1,0:T(1,128)S(1)} all-to-all(f32[32,1,384]{2,1,0:T(1,128)S(1)} %get-tuple-element.16), channel_id=1, replica_groups=mesh['dom'=8,'sub'=4] {'dom','sub'}, dimensions={0} | all-to-all | bytes 98304 | tf_op jit(solution)/shard_map/all_to_all | solution.py:409
  15.7 0.0 copy-done
  15.7 3.2 %gradient.2 = (f32[3,16,128]{2,1,0:T(8,128)S(1)}, f32[32,1,384]{2,1,0:T(1,128)S(1)}) custom-call(f32[3,2048]{1,0:T(4,128)S(1)} %copy-done, f32[32,1,384]{2,1,0:T(1,128)S(1)} %all_to_all.20.ghost_ref, s32[64,128]{1,0:T(8,128)S(1)} %get-tuple-element.17.pair_nodes_ref, s32[64,128]{1,0:T(8,128)S(1)} %get-tuple-element.18.block_nodes_ref, ...), custom_call_target="tpu_custom_call" | custom-call | tf_op jit(solution)/shard_map/gradient/pallas_call | solution.py:416
  18.8 0.0 copy-start.1
  18.9 0.0 copy-start.2
  18.9 9.0 %all_to_all.21.back_ref = f32[32,1,384]{2,1,0:T(1,128)S(1)} all-to-all(f32[32,1,384]{2,1,0:T(1,128)S(1)} %get-tuple-element.21), channel_id=1, replica_groups=mesh['dom'=8,'sub'=4] {'dom','sub'}, dimensions={0} | all-to-all | bytes 98304 | tf_op jit(solution)/shard_map/all_to_all | solution.py:409
  27.9 0.0 copy-done.1
  27.9 0.0 copy-done.2
  27.9 0.6 %move.1 = (f32[3,2048]{1,0:T(4,128)S(1)}, f32[32,1,384]{2,1,0:T(1,128)S(1)}) custom-call(f32[3,2048]{1,0:T(4,128)S(1)} %copy-done, s32[16,128]{1,0:T(8,128)S(1)} %bitcast.11, f32[3,16,128]{2,1,0:T(8,128)S(1)} %get-tuple-element.20.own_ref, f32[32,1,384]{2,1,0:T(1,128)S(1)} %all_to_all.21.back_ref, s32[5,4,128]{2,1,0:T(4,128)S(1)} %bitcast.9, ...), custom_call_target="tpu_custom_call" | custom-call | tf_op jit(solution)/shard_map/move/pallas_call | solution.py:425
  28.5 9.0 %all_to_all.22.ghost_ref = f32[32,1,384]{2,1,0:T(1,128)S(1)} all-to-all(f32[32,1,384]{2,1,0:T(1,128)S(1)} %get-tuple-element.24), channel_id=1, replica_groups=mesh['dom'=8,'sub'=4] {'dom','sub'}, dimensions={0} | all-to-all | bytes 98304 | tf_op jit(solution)/shard_map/all_to_all | solution.py:409
  37.5 3.2 %gradient.3 = (f32[3,16,128]{2,1,0:T(8,128)S(1)}, f32[32,1,384]{2,1,0:T(1,128)S(1)}) custom-call(f32[3,2048]{1,0:T(4,128)S(1)} %get-tuple-element.23.positions_ref, f32[32,1,384]{2,1,0:T(1,128)S(1)} %all_to_all.22.ghost_ref, s32[64,128]{1,0:T(8,128)S(1)} %get-tuple-element.17.pair_nodes_ref, s32[64,128]{1,0:T(8,128)S(1)} %get-tuple-element.18.block_nodes_ref, ...), custom_call_target="tpu_custom_call" | custom-call | tf_op jit(solution)/shard_map/gradient/pallas_call | solution.py:416
  40.7 9.0 %all_to_all.23.back_ref = f32[32,1,384]{2,1,0:T(1,128)S(1)} all-to-all(f32[32,1,384]{2,1,0:T(1,128)S(1)} %get-tuple-element.26), channel_id=1, replica_groups=mesh['dom'=8,'sub'=4] {'dom','sub'}, dimensions={0} | all-to-all | bytes 98304 | tf_op jit(solution)/shard_map/all_to_all | solution.py:409
  49.7 1.0 %move_last.1 = f32[3,2048]{1,0:T(4,128)} custom-call(f32[3,2048]{1,0:T(4,128)S(1)} %get-tuple-element.23.positions_ref, s32[16,128]{1,0:T(8,128)S(1)} %bitcast.12, f32[3,16,128]{2,1,0:T(8,128)S(1)} %get-tuple-element.25.own_ref, f32[32,1,384]{2,1,0:T(1,128)S(1)} %all_to_all.23.back_ref, s32[5,4,128]{2,1,0:T(4,128)S(1)} %bitcast.10, ...), custom_call_target="tpu_custom_call" | custom-call | tf_op jit(solution)/shard_map/move_last/pallas_call | solution.py:425
Async XLA Ops:
  1.2 14.5 %copy-start = (f32[3,2048]{1,0:T(4,128)S(1)}, f32[3,2048]{1,0:T(4,128)}, u32[]{:S(2)}) copy-start(f32[3,2048]{1,0:T(4,128)} %positions_ref.3) | copy-start | bytes 73732
  18.8 9.1 %copy-start.1 = (s32[1,1,5,4,128]{4,3,2,1,0:T(4,128)S(1)}, s32[1,1,5,4,128]{4,3,2,1,0:T(4,128)}, u32[]{:S(2)}) copy-start(s32[1,1,5,4,128]{4,3,2,1,0:T(4,128)} %param.9) | copy-start | bytes 30724
  18.9 9.0 %copy-start.2 = (s32[2048]{0:T(1024)S(1)}, s32[2048]{0:T(1024)}, u32[]{:S(2)}) copy-start(s32[2048]{0:T(1024)} %param.7) | copy-start | bytes 24580

commit v6 on v5

--- a/solution.py
+++ b/solution.py
@@ -48,9 +48,13 @@
     return jnp.where(mask, jnp.full((rows, LANES), value, jnp.bfloat16), jnp.zeros((rows, LANES), jnp.bfloat16))
 
 
-def split_two(values):
-    upper = values.astype(jnp.bfloat16).astype(jnp.float32)
-    return upper, values - upper
+def split(values, count):
+    parts = []
+    for _ in range(count - 1):
+        upper = values.astype(jnp.bfloat16).astype(jnp.float32)
+        parts.append(upper)
+        values = values - upper
+    return parts + [values]
 
 
 def masked_rows(mask, row):
@@ -206,7 +210,7 @@
     return jnp.concatenate(tiles, axis=0), place
 
 
-def column_sums(node_ref, pair_nodes_ref, block_nodes_ref, rows):
+def column_sums(node_ref, pair_nodes_ref, block_nodes_ref, rows, splits):
     pair_count = pair_nodes_ref.shape[0]
     left, right = [], []
     place = None
@@ -215,7 +219,7 @@
     lanes = [(lane + i * LANES).astype(jnp.int16) for i in range(2)]
     ones = jnp.ones((BLOCK_ROWS, LANES), jnp.bfloat16)
     for p in range(pair_count):
-        parts = [part[r : r + 1, :] for part in split_two(node_ref[p * 8 : (p + 1) * 8, :]) for r in range(3)]
+        parts = [part[r : r + 1, :] for part in split(node_ref[p * 8 : (p + 1) * 8, :], splits) for r in range(3)]
         high = pair_nodes_ref[p : p + 1, :] >> 8
         spread, place = spread_rows(high.astype(jnp.float32), parts, -(-rows // 2))
         left.append(spread)
@@ -231,16 +235,16 @@
     )
 
     def row(r, h):
-        upper, lower = place[r, h // 2], place[3 + r, h // 2]
         half = slice((h % 2) * LANES, (h % 2 + 1) * LANES)
-        return total[upper : upper + 1, half] + total[lower : lower + 1, half]
+        return sum(total[i : i + 1, half] for i in (place[3 * s + r, h // 2] for s in range(splits)))
 
     return row
 
 
 def gradient_kernel(
-    positions_ref, ghost_ref, pair_nodes_ref, block_nodes_ref, corner_ref, own_ref, back_ref, terms_ref, node_ref, *, dom_count, slot_count
+    positions_ref, ghost_ref, pair_nodes_ref, block_nodes_ref, corner_ref, own_ref, back_ref, terms_ref, node_ref, *, dom_count, slot_count, splits
 ):
+    part_rows = terms_ref.shape[1] // pair_nodes_ref.shape[0]
     owned_rows = own_ref.shape[1]
     dom_here = lax.axis_index("dom")
     sub_count = ghost_ref.shape[0] // dom_count
@@ -270,11 +274,12 @@
             gradient = distortion_gradient(corners)
             for r in range(3):
                 for m in range(3):
-                    for s, part in enumerate(split_two(gradient[r][m + 1])):
-                        terms_ref[m * 2 + q, pl.ds(g * 64 + s * 4 + r, 8, stride=8), :] = part
+                    for s, part in enumerate(split(gradient[r][m + 1], splits)):
+                        first = g * 8 * part_rows + s * 4 + r
+                        terms_ref[m * 2 + q, pl.ds(first, 8, stride=part_rows), :] = part
 
     def add_tets(p):
-        empty = jnp.zeros((8, LANES), jnp.float32)
+        empty = jnp.zeros((part_rows, LANES), jnp.float32)
         blocks = [p, pair_count + p]
         base = [one_hot(corner_ref[b, 0:1, :], BLOCK_ROWS, -1.0) for b in blocks]
         hits, terms = [], []
@@ -282,19 +287,20 @@
             for q in range(2):
                 hit = row_equals(corner_ref[blocks[q], m + 1 : m + 2, :], BLOCK_ROWS)
                 hits.append(jnp.where(hit, jnp.ones_like(base[q]), base[q]))
-                part = terms_ref[m * 2 + q, p * 8 : (p + 1) * 8, :]
+                part = terms_ref[m * 2 + q, p * part_rows : (p + 1) * part_rows, :]
                 part = jnp.concatenate([part, empty] if q == 0 else [empty, part], axis=0)
                 terms.append(part.astype(jnp.bfloat16))
         sums = contract_lanes(jnp.concatenate(terms, axis=1), jnp.concatenate(hits, axis=1))
-        sums = jnp.concatenate([sums[:8], sums[8:]], axis=1)
-        node_ref[p * 8 : (p + 1) * 8, :] = sums + pltpu.roll(sums, 4, 0)
+        sums = jnp.concatenate([sums[:part_rows], sums[part_rows:]], axis=1)
+        node = sums[:8] + pltpu.roll(sums[:8], 4, 0)
+        node_ref[p * 8 : (p + 1) * 8, :] = node + sums[8:] if part_rows > 8 else node
 
     for g in range(pair_count // 8):
         tets_of_pairs(g)
     for p in range(pair_count):
         add_tets(p)
     back_ref[...] = jnp.zeros(back_ref.shape, jnp.float32)
-    row = column_sums(node_ref, pair_nodes_ref, block_nodes_ref, owned_rows + ghost_rows)
+    row = column_sums(node_ref, pair_nodes_ref, block_nodes_ref, owned_rows + ghost_rows, splits)
     for r in range(3):
         for h in range(owned_rows):
             own_ref[r, h : h + 1, :] = row(r, h)
@@ -304,7 +310,7 @@
                 back_ref[pl.ds(place, 1), 0, r * LANES : (r + 1) * LANES] = row(r, owned_rows + k * sub_count + t)
 
 
-def moved_positions(positions_ref, mask_ref, own_ref, back_ref, list_ref, valid_ref, dom_count):
+def moved_positions(positions_ref, mask_ref, own_ref, back_ref, list_ref, valid_ref, dom_count, splits):
     dom_here = lax.axis_index("dom")
     slot_count, sub_count, width = list_ref.shape
     reach = (slot_count - 1) // 2
@@ -319,14 +325,14 @@
             parts = []
             for r in range(3):
                 row = back_ref[pl.ds(source + t, 1), 0, r * LANES : (r + 1) * LANES]
-                parts.append(split_two(jnp.where(valid, row, 0.0)))
-            left.append(jnp.concatenate([masked_rows(mask, parts[r][s]) for s in range(2) for r in range(3)], axis=0))
+                parts.append(split(jnp.where(valid, row, 0.0), splits))
+            left.append(jnp.concatenate([masked_rows(mask, parts[r][s]) for s in range(splits) for r in range(3)], axis=0))
             right.append(one_hot(index & (LANES - 1), LANES))
     returned = contract_lanes(jnp.concatenate(left, axis=1), jnp.concatenate(right, axis=1))
     free = jnp.where(mask_ref[...] == 0, step_size, 0.0)
     moved = []
     for r in range(3):
-        added = returned[r * owned_rows : (r + 1) * owned_rows] + returned[(3 + r) * owned_rows : (4 + r) * owned_rows]
+        added = sum(returned[i * owned_rows : (i + 1) * owned_rows] for i in range(r, 3 * splits, 3))
         here = jnp.concatenate(
             [positions_ref[r : r + 1, h * LANES : (h + 1) * LANES] for h in range(owned_rows)], axis=0
         )
@@ -334,8 +340,8 @@
     return moved
 
 
-def move_kernel(positions_ref, mask_ref, own_ref, back_ref, list_ref, valid_ref, *out_refs, dom_count):
-    moved = moved_positions(positions_ref, mask_ref, own_ref, back_ref, list_ref, valid_ref, dom_count)
+def move_kernel(positions_ref, mask_ref, own_ref, back_ref, list_ref, valid_ref, *out_refs, dom_count, splits):
+    moved = moved_positions(positions_ref, mask_ref, own_ref, back_ref, list_ref, valid_ref, dom_count, splits)
     owned_rows = own_ref.shape[1]
     for r in range(3):
         for h in range(owned_rows):
@@ -392,18 +398,6 @@
         dom_count=dom_count,
     )
     own_shape = jax.ShapeDtypeStruct((3, owned_rows, LANES), jnp.float32)
-    gradient = call(
-        gradient_kernel,
-        "gradient",
-        [vmem] * 5,
-        (own_shape, exchange_shape),
-        [
-            pltpu.VMEM((6, block_count * 4, LANES), jnp.float32),
-            pltpu.VMEM((block_count * 4, LANES), jnp.float32),
-        ],
-        dom_count=dom_count,
-        slot_count=slot_count,
-    )
 
     def exchange(rows):
         return lax.all_to_all(rows, ("dom", "sub"), 0, 0, tiled=True)
@@ -413,6 +407,20 @@
     for step in range(ITERS):
         last = step == ITERS - 1
         ghosts = exchange(payload)
+        splits = 2 if last else 3
+        gradient = call(
+            gradient_kernel,
+            "gradient_last" if last else "gradient",
+            [vmem] * 5,
+            (own_shape, exchange_shape),
+            [
+                pltpu.VMEM((6, block_count * (4 if last else 8), LANES), jnp.float32),
+                pltpu.VMEM((block_count * 4, LANES), jnp.float32),
+            ],
+            dom_count=dom_count,
+            slot_count=slot_count,
+            splits=splits,
+        )
         own, back = gradient(positions, ghosts, pair_nodes, block_nodes, corners)
         returned = exchange(back)
         move = call(
@@ -421,6 +429,7 @@
             [vmem] * 6,
             (position_shape,) if last else (position_shape, exchange_shape),
             dom_count=dom_count,
+            splits=splits,
         )
         moved = move(positions, mask_rows, own, returned, lists, valid)
         positions = moved[0]

time: 51 us -> 51.8 us (1.016)
  Pallas kernels: 9.13 us -> 9.89 us
    pallas_call x2, Pallas kernels: 6.32 us -> 7.06 us  [per_device(): own, back = gradient(positions, ghosts, pair_nodes, block_nodes, corners)]
where the time goes in v6:
time: 51.8 us; the launch traced here: 51.5 us
  blocking collectives  41.5 us (80%)
  Pallas kernels  9.89 us (19%)
    all_to_all x4, blocking collectives, exchange(): return lax.all_to_all(rows, ('dom', 'sub'), 0, 0, tiled=True)  41.5 us
    pallas_call x2, Pallas kernels, per_device(): own, back = gradient(positions, ghosts, pair_nodes, block_nodes, corners)  7.06 us
    pallas_call x2, Pallas kernels, per_device(): moved = move(positions, mask_rows, own, returned, lists, valid)  1.61 us
    pallas_call x1, Pallas kernels, per_device(): send(*[pltpu.with_memory_space_constraint(x, pltpu.HBM) for x in inputs])  1.21 us

profile of v6, /device:TPU:0, one launch (start us, length us, event | category | flops | bytes accessed | tf_op | source)
XLA Modules:
  0.0 51.5 jit_solution(16880549331598655599)
XLA Ops:
  0.0 1.2 %send.1 = (f32[32,1,384]{2,1,0:T(1,128)S(1)}, f32[5,4,128]{2,1,0:T(4,128)S(1)}, s32[64,128]{1,0:T(8,128)S(1)}, s32[64,128]{1,0:T(8,128)S(1)}, s32[128,4,128]{2,1,0:T(4,128)S(1)}) custom-call(f32[3,2048]{1,0:T(4,128)} %positions_ref.3, s32[5,4,128]{2,1,0:T(4,128)} %bitcast.8, s32[4,5]{1,0:T(4,128)} %bitcast.14, s32[64,128]{1,0:T(8,128)} %block_nodes_hbm.1, ...), custom_call_target="tpu_custom_call" | custom-call | tf_op jit(solution)/shard_map/send/pallas_call | solution.py:406
  1.2 0.0 copy-start
  1.2 14.4 %all_to_all.20.ghost_ref = f32[32,1,384]{2,1,0:T(1,128)S(1)} all-to-all(f32[32,1,384]{2,1,0:T(1,128)S(1)} %get-tuple-element.16), channel_id=1, replica_groups=mesh['dom'=8,'sub'=4] {'dom','sub'}, dimensions={0} | all-to-all | bytes 98304 | tf_op jit(solution)/shard_map/all_to_all | solution.py:403
  15.7 0.0 copy-done
  15.7 3.9 %gradient.1 = (f32[3,16,128]{2,1,0:T(8,128)S(1)}, f32[32,1,384]{2,1,0:T(1,128)S(1)}) custom-call(f32[3,2048]{1,0:T(4,128)S(1)} %copy-done, f32[32,1,384]{2,1,0:T(1,128)S(1)} %all_to_all.20.ghost_ref, s32[64,128]{1,0:T(8,128)S(1)} %get-tuple-element.17.pair_nodes_ref, s32[64,128]{1,0:T(8,128)S(1)} %get-tuple-element.18.block_nodes_ref, ...), custom_call_target="tpu_custom_call" | custom-call | tf_op jit(solution)/shard_map/gradient/pallas_call | solution.py:424
  19.6 0.0 copy-start.1
  19.6 0.0 copy-start.2
  19.6 9.0 %all_to_all.21.back_ref = f32[32,1,384]{2,1,0:T(1,128)S(1)} all-to-all(f32[32,1,384]{2,1,0:T(1,128)S(1)} %get-tuple-element.21), channel_id=1, replica_groups=mesh['dom'=8,'sub'=4] {'dom','sub'}, dimensions={0} | all-to-all | bytes 98304 | tf_op jit(solution)/shard_map/all_to_all | solution.py:403
  28.6 0.0 copy-done.1
  28.6 0.0 copy-done.2
  28.6 0.6 %move.1 = (f32[3,2048]{1,0:T(4,128)S(1)}, f32[32,1,384]{2,1,0:T(1,128)S(1)}) custom-call(f32[3,2048]{1,0:T(4,128)S(1)} %copy-done, s32[16,128]{1,0:T(8,128)S(1)} %bitcast.11, f32[3,16,128]{2,1,0:T(8,128)S(1)} %get-tuple-element.20.own_ref, f32[32,1,384]{2,1,0:T(1,128)S(1)} %all_to_all.21.back_ref, s32[5,4,128]{2,1,0:T(4,128)S(1)} %bitcast.9, ...), custom_call_target="tpu_custom_call" | custom-call | tf_op jit(solution)/shard_map/move/pallas_call | solution.py:434
  29.3 9.0 %all_to_all.22.ghost_ref = f32[32,1,384]{2,1,0:T(1,128)S(1)} all-to-all(f32[32,1,384]{2,1,0:T(1,128)S(1)} %get-tuple-element.24), channel_id=1, replica_groups=mesh['dom'=8,'sub'=4] {'dom','sub'}, dimensions={0} | all-to-all | bytes 98304 | tf_op jit(solution)/shard_map/all_to_all | solution.py:403
  38.3 3.2 %gradient_last.1 = (f32[3,16,128]{2,1,0:T(8,128)S(1)}, f32[32,1,384]{2,1,0:T(1,128)S(1)}) custom-call(f32[3,2048]{1,0:T(4,128)S(1)} %get-tuple-element.23.positions_ref, f32[32,1,384]{2,1,0:T(1,128)S(1)} %all_to_all.22.ghost_ref, s32[64,128]{1,0:T(8,128)S(1)} %get-tuple-element.17.pair_nodes_ref, s32[64,128]{1,0:T(8,128)S(1)} %get-tuple-element.18.block_nodes_ref, ...), custom_call_target="tpu_custom_call" | custom-call | tf_op jit(solution)/shard_map/gradient_last/pallas_call | solution.py:424
  41.5 9.0 %all_to_all.23.back_ref = f32[32,1,384]{2,1,0:T(1,128)S(1)} all-to-all(f32[32,1,384]{2,1,0:T(1,128)S(1)} %get-tuple-element.26), channel_id=1, replica_groups=mesh['dom'=8,'sub'=4] {'dom','sub'}, dimensions={0} | all-to-all | bytes 98304 | tf_op jit(solution)/shard_map/all_to_all | solution.py:403
  50.5 1.0 %move_last.1 = f32[3,2048]{1,0:T(4,128)} custom-call(f32[3,2048]{1,0:T(4,128)S(1)} %get-tuple-element.23.positions_ref, s32[16,128]{1,0:T(8,128)S(1)} %bitcast.12, f32[3,16,128]{2,1,0:T(8,128)S(1)} %get-tuple-element.25.own_ref, f32[32,1,384]{2,1,0:T(1,128)S(1)} %all_to_all.23.back_ref, s32[5,4,128]{2,1,0:T(4,128)S(1)} %bitcast.10, ...), custom_call_target="tpu_custom_call" | custom-call | tf_op jit(solution)/shard_map/move_last/pallas_call | solution.py:434
Async XLA Ops:
  1.2 14.5 %copy-start = (f32[3,2048]{1,0:T(4,128)S(1)}, f32[3,2048]{1,0:T(4,128)}, u32[]{:S(2)}) copy-start(f32[3,2048]{1,0:T(4,128)} %positions_ref.3) | copy-start | bytes 73732
  19.6 9.1 %copy-start.1 = (s32[1,1,5,4,128]{4,3,2,1,0:T(4,128)S(1)}, s32[1,1,5,4,128]{4,3,2,1,0:T(4,128)}, u32[]{:S(2)}) copy-start(s32[1,1,5,4,128]{4,3,2,1,0:T(4,128)} %param.9) | copy-start | bytes 30724
  19.6 9.0 %copy-start.2 = (s32[2048]{0:T(1024)S(1)}, s32[2048]{0:T(1024)}, u32[]{:S(2)}) copy-start(s32[2048]{0:T(1024)} %param.7) | copy-start | bytes 24580

commit v7 on v6

--- a/solution.py
+++ b/solution.py
@@ -118,7 +118,6 @@
     dom_here = lax.axis_index("dom")
     slot_count, sub_count, width = list_ref.shape
     reach = (slot_count - 1) // 2
-    out_ref[...] = jnp.zeros(out_ref.shape, jnp.float32)
     group = max(1, 8 // sub_count)
     for first in range(0, slot_count, group):
         slots = range(first, min(first + group, slot_count))
@@ -166,7 +165,8 @@
     ]
     for copy in copies:
         copy.start()
-    for copy in copies[:3]:
+    out_ref[...] = jnp.zeros(out_ref.shape, jnp.float32)
+    for copy in copies[:4]:
         copy.wait()
     slot_count, sub_count, width = list_ref.shape
     lane = lax.broadcasted_iota(jnp.int32, (sub_count, LANES), 1)
@@ -176,7 +176,6 @@
     write_payload(
         position_row(positions_ref), positions_ref.shape[1] // LANES, list_ref, valid_ref, out_ref, dom_count
     )
-    copies[3].wait()
     half = pair_nodes_ref.shape[0]
     nodes = block_nodes_ref[...].T
     pair_nodes_ref[...] = jnp.concatenate([nodes[:half], nodes[half:]], axis=1)
@@ -347,6 +346,7 @@
         for h in range(owned_rows):
             out_refs[0][r : r + 1, h * LANES : (h + 1) * LANES] = moved[r][h : h + 1]
     if len(out_refs) > 1:
+        out_refs[1][...] = jnp.zeros(out_refs[1].shape, jnp.float32)
         write_payload(lambda r, h: moved[r][h : h + 1], owned_rows, list_ref, valid_ref, out_refs[1], dom_count)
 
 

time: 51.8 us -> 51.7 us (level)
  no operation moved by 1% of the time
where the time goes in v7:
time: 51.7 us; the launch traced here: 51.5 us
  blocking collectives  41.5 us (80%)
  Pallas kernels  9.86 us (19%)
    all_to_all x4, blocking collectives, exchange(): return lax.all_to_all(rows, ('dom', 'sub'), 0, 0, tiled=True)  41.5 us
    pallas_call x2, Pallas kernels, per_device(): own, back = gradient(positions, ghosts, pair_nodes, block_nodes, corners)  7.05 us
    pallas_call x2, Pallas kernels, per_device(): moved = move(positions, mask_rows, own, returned, lists, valid)  1.61 us
    pallas_call x1, Pallas kernels, per_device(): send(*[pltpu.with_memory_space_constraint(x, pltpu.HBM) for x in inputs])  1.19 us

profile of v7, /device:TPU:0, one launch (start us, length us, event | category | flops | bytes accessed | tf_op | source)
XLA Modules:
  0.0 51.5 jit_solution(8343119093393461906)
XLA Ops:
  0.0 1.2 %send.1 = (f32[32,1,384]{2,1,0:T(1,128)S(1)}, f32[5,4,128]{2,1,0:T(4,128)S(1)}, s32[64,128]{1,0:T(8,128)S(1)}, s32[64,128]{1,0:T(8,128)S(1)}, s32[128,4,128]{2,1,0:T(4,128)S(1)}) custom-call(f32[3,2048]{1,0:T(4,128)} %positions_ref.3, s32[5,4,128]{2,1,0:T(4,128)} %bitcast.8, s32[4,5]{1,0:T(4,128)} %bitcast.14, s32[64,128]{1,0:T(8,128)} %block_nodes_hbm.1, ...), custom_call_target="tpu_custom_call" | custom-call | tf_op jit(solution)/shard_map/send/pallas_call | solution.py:406
  1.2 0.0 copy-start
  1.2 14.4 %all_to_all.20.ghost_ref = f32[32,1,384]{2,1,0:T(1,128)S(1)} all-to-all(f32[32,1,384]{2,1,0:T(1,128)S(1)} %get-tuple-element.16), channel_id=1, replica_groups=mesh['dom'=8,'sub'=4] {'dom','sub'}, dimensions={0} | all-to-all | bytes 98304 | tf_op jit(solution)/shard_map/all_to_all | solution.py:403
  15.7 0.0 copy-done
  15.7 3.9 %gradient.1 = (f32[3,16,128]{2,1,0:T(8,128)S(1)}, f32[32,1,384]{2,1,0:T(1,128)S(1)}) custom-call(f32[3,2048]{1,0:T(4,128)S(1)} %copy-done, f32[32,1,384]{2,1,0:T(1,128)S(1)} %all_to_all.20.ghost_ref, s32[64,128]{1,0:T(8,128)S(1)} %get-tuple-element.17.pair_nodes_ref, s32[64,128]{1,0:T(8,128)S(1)} %get-tuple-element.18.block_nodes_ref, ...), custom_call_target="tpu_custom_call" | custom-call | tf_op jit(solution)/shard_map/gradient/pallas_call | solution.py:424
  19.6 0.0 copy-start.1
  19.6 0.0 copy-start.2
  19.6 9.0 %all_to_all.21.back_ref = f32[32,1,384]{2,1,0:T(1,128)S(1)} all-to-all(f32[32,1,384]{2,1,0:T(1,128)S(1)} %get-tuple-element.21), channel_id=1, replica_groups=mesh['dom'=8,'sub'=4] {'dom','sub'}, dimensions={0} | all-to-all | bytes 98304 | tf_op jit(solution)/shard_map/all_to_all | solution.py:403
  28.6 0.0 copy-done.1
  28.6 0.0 copy-done.2
  28.6 0.6 %move.1 = (f32[3,2048]{1,0:T(4,128)S(1)}, f32[32,1,384]{2,1,0:T(1,128)S(1)}) custom-call(f32[3,2048]{1,0:T(4,128)S(1)} %copy-done, s32[16,128]{1,0:T(8,128)S(1)} %bitcast.11, f32[3,16,128]{2,1,0:T(8,128)S(1)} %get-tuple-element.20.own_ref, f32[32,1,384]{2,1,0:T(1,128)S(1)} %all_to_all.21.back_ref, s32[5,4,128]{2,1,0:T(4,128)S(1)} %bitcast.9, ...), custom_call_target="tpu_custom_call" | custom-call | tf_op jit(solution)/shard_map/move/pallas_call | solution.py:434
  29.3 9.0 %all_to_all.22.ghost_ref = f32[32,1,384]{2,1,0:T(1,128)S(1)} all-to-all(f32[32,1,384]{2,1,0:T(1,128)S(1)} %get-tuple-element.24), channel_id=1, replica_groups=mesh['dom'=8,'sub'=4] {'dom','sub'}, dimensions={0} | all-to-all | bytes 98304 | tf_op jit(solution)/shard_map/all_to_all | solution.py:403
  38.3 3.2 %gradient_last.1 = (f32[3,16,128]{2,1,0:T(8,128)S(1)}, f32[32,1,384]{2,1,0:T(1,128)S(1)}) custom-call(f32[3,2048]{1,0:T(4,128)S(1)} %get-tuple-element.23.positions_ref, f32[32,1,384]{2,1,0:T(1,128)S(1)} %all_to_all.22.ghost_ref, s32[64,128]{1,0:T(8,128)S(1)} %get-tuple-element.17.pair_nodes_ref, s32[64,128]{1,0:T(8,128)S(1)} %get-tuple-element.18.block_nodes_ref, ...), custom_call_target="tpu_custom_call" | custom-call | tf_op jit(solution)/shard_map/gradient_last/pallas_call | solution.py:424
  41.4 9.0 %all_to_all.23.back_ref = f32[32,1,384]{2,1,0:T(1,128)S(1)} all-to-all(f32[32,1,384]{2,1,0:T(1,128)S(1)} %get-tuple-element.26), channel_id=1, replica_groups=mesh['dom'=8,'sub'=4] {'dom','sub'}, dimensions={0} | all-to-all | bytes 98304 | tf_op jit(solution)/shard_map/all_to_all | solution.py:403
  50.5 1.0 %move_last.1 = f32[3,2048]{1,0:T(4,128)} custom-call(f32[3,2048]{1,0:T(4,128)S(1)} %get-tuple-element.23.positions_ref, s32[16,128]{1,0:T(8,128)S(1)} %bitcast.12, f32[3,16,128]{2,1,0:T(8,128)S(1)} %get-tuple-element.25.own_ref, f32[32,1,384]{2,1,0:T(1,128)S(1)} %all_to_all.23.back_ref, s32[5,4,128]{2,1,0:T(4,128)S(1)} %bitcast.10, ...), custom_call_target="tpu_custom_call" | custom-call | tf_op jit(solution)/shard_map/move_last/pallas_call | solution.py:434
Async XLA Ops:
  1.2 14.5 %copy-start = (f32[3,2048]{1,0:T(4,128)S(1)}, f32[3,2048]{1,0:T(4,128)}, u32[]{:S(2)}) copy-start(f32[3,2048]{1,0:T(4,128)} %positions_ref.3) | copy-start | bytes 73732
  19.6 9.1 %copy-start.1 = (s32[1,1,5,4,128]{4,3,2,1,0:T(4,128)S(1)}, s32[1,1,5,4,128]{4,3,2,1,0:T(4,128)}, u32[]{:S(2)}) copy-start(s32[1,1,5,4,128]{4,3,2,1,0:T(4,128)} %param.9) | copy-start | bytes 30724
  19.6 9.0 %copy-start.2 = (s32[2048]{0:T(1024)S(1)}, s32[2048]{0:T(1024)}, u32[]{:S(2)}) copy-start(s32[2048]{0:T(1024)} %param.7) | copy-start | bytes 24580
